TPU v7x, 512 devices: a whole 4x8x8 slice. The times are simulated.
512 devices in a mesh: grp: 4 (over x), row: 128 (over y, z, core).
Axes of the slice: x: 4, y: 8, z: 8, core: 2. Of those that a mesh axis runs over, the one named last changes fastest.
Arguments:
- sketch: float32 [393216, 512], P('row', 'grp'), may hold values from -600 to 600, as said below
Outputs:
- basis: float32 [393216, 512], P(('row', 'grp'))
- upper: float32 [512, 512], replicated
Inputs may be any that keep to these rules, and one draw needn't show every extreme that they name: `sketch`: real values, the columns linearly independent.
All inputs are finite; a program needn't handle non-finite values.
Results may differ from a plain program's by a relative error of at most 0.000075.
Values sent between devices are 32-bit elements; how exact they have to be, the bound alone decides.
No kernel may reach another device: no remote copies, remote signals or barrier semaphores. Data moves between devices by JAX's collectives and lax.ppermute only.
A program may use at most 128 MiB of HBM per device.

v0:
```python
import jax
import jax.numpy as jnp
from jax import lax
from jax.sharding import PartitionSpec as P


def partner(block, axis, distance):
    count = lax.axis_size(axis)
    route = []
    for low in range(count):
        high = low | 1 << distance
        if high != low and high < count:
            route += [(low, high), (high, low)]
    return lax.ppermute(block, axis, route)


def matmul(left, right):
    return jnp.dot(left, right, precision=lax.Precision.HIGHEST, preferred_element_type=jnp.float32)


def factor_pair(matrix):
    count = matrix.shape[0]
    if count == 1:
        root = jnp.sqrt(matrix)
        return (root, 1.0 / root)
    half = count // 2
    lower_top, inv_top = factor_pair(matrix[:half, :half])
    below = matmul(matrix[half:, :half], inv_top.T)
    schur = matrix[half:, half:] - matmul(below, below.T)
    lower_bottom, inv_bottom = factor_pair(schur)
    corner = -matmul(inv_bottom, matmul(below, inv_top))
    zeros_top = jnp.zeros((half, count - half), jnp.float32)
    lower = jnp.concatenate(
        [
            jnp.concatenate([lower_top, zeros_top], axis=1),
            jnp.concatenate([below, lower_bottom], axis=1),
        ],
        axis=0,
    )
    inverse = jnp.concatenate(
        [
            jnp.concatenate([inv_top, zeros_top], axis=1),
            jnp.concatenate([corner, inv_bottom], axis=1),
        ],
        axis=0,
    )
    return (lower, inverse)


def local(sketch):
    block = lax.all_to_all(sketch, "grp", split_axis=0, concat_axis=1, tiled=True)
    devices = lax.axis_size(("grp", "row"))
    total_rows = block.shape[0] * devices
    partial_gram = lax.dot_general(
        block,
        block,
        (((0,), (0,)), ((), ())),
        precision=lax.Precision.HIGHEST,
        preferred_element_type=jnp.float32,
    ) / jnp.float32(total_rows)
    gram = partial_gram
    for section in range(devices.bit_length() - 1):
        gram = gram + partner(gram, ("grp", "row"), section)
    lower, lower_inverse = factor_pair(gram)
    upper = lower.T
    basis = matmul(block, lower_inverse.T)
    return (basis, upper)


def solution(mesh):
    return jax.shard_map(
        local,
        mesh=mesh,
        in_specs=(P("row", "grp"),),
        out_specs=(P(("row", "grp"), None), P()),
        check_vma=False,
    )
```

profile of v0, /device:TPU:1, one launch (start us, length us, event | category | flops | bytes accessed | tf_op | source)
XLA Modules:
  0.0 1547.5 jit_solution(10468469932017566789)
XLA Ops:
  0.6 19.7 %all_to_all.19 = f32[4,768,128]{2,1,0:T(8,128)S(1)} all-to-all(f32[4,768,128]{2,1,0:T(8,128)} %bitcast.3079), channel_id=1, replica_groups=mesh['grp'=4,'row'=128] {'grp'}, dimensions={0} | all-to-all | bytes 3145728 | tf_op jit(solution)/shard_map/all_to_all | solution.py:51
  20.8 2.7 convolution_multiply_fusion
  23.5 8.7 collective-permute-start
  32.2 2.3 collective-permute-done
  34.7 4.0 collective-permute-start.1
  38.7 23.2 %collective-permute-done.1 = f32[512,512]{0,1:T(8,128)S(1)} collective-permute-done((f32[512,512]{0,1:T(8,128)S(1)}, f32[512,512]{0,1:T(8,128)S(1)}, u32[]{:S(2)}, u32[]{:S(2)}) %collective-permute-start.1) | collective-permute-done | bytes 1048608 | tf_op jit(solution)/shard_map/ppermute | solution.py:14
  62.1 5.8 collective-permute-start.2
  68.0 45.2 %collective-permute-done.2 = f32[512,512]{0,1:T(8,128)S(1)} collective-permute-done((f32[512,512]{0,1:T(8,128)S(1)}, f32[512,512]{0,1:T(8,128)S(1)}, u32[]{:S(2)}, u32[]{:S(2)}) %collective-permute-start.2) | collective-permute-done | bytes 1048608 | tf_op jit(solution)/shard_map/ppermute | solution.py:14
  113.4 8.0 collective-permute-start.3
  121.4 44.9 %collective-permute-done.3 = f32[512,512]{0,1:T(8,128)S(1)} collective-permute-done((f32[512,512]{0,1:T(8,128)S(1)}, f32[512,512]{0,1:T(8,128)S(1)}, u32[]{:S(2)}, u32[]{:S(2)}) %collective-permute-start.3) | collective-permute-done | bytes 1048608 | tf_op jit(solution)/shard_map/ppermute | solution.py:14
  166.5 3.2 collective-permute-start.4
  169.7 21.2 %collective-permute-done.4 = f32[512,512]{0,1:T(8,128)S(1)} collective-permute-done((f32[512,512]{0,1:T(8,128)S(1)}, f32[512,512]{0,1:T(8,128)S(1)}, u32[]{:S(2)}, u32[]{:S(2)}) %collective-permute-start.4) | collective-permute-done | bytes 1048608 | tf_op jit(solution)/shard_map/ppermute | solution.py:14
  191.1 4.2 collective-permute-start.5
  195.3 45.0 %collective-permute-done.5 = f32[512,512]{0,1:T(8,128)S(1)} collective-permute-done((f32[512,512]{0,1:T(8,128)S(1)}, f32[512,512]{0,1:T(8,128)S(1)}, u32[]{:S(2)}, u32[]{:S(2)}) %collective-permute-start.5) | collective-permute-done | bytes 1048608 | tf_op jit(solution)/shard_map/ppermute | solution.py:14
  240.5 8.4 collective-permute-start.6
  249.0 45.7 %collective-permute-done.6 = f32[512,512]{0,1:T(8,128)S(1)} collective-permute-done((f32[512,512]{0,1:T(8,128)S(1)}, f32[512,512]{0,1:T(8,128)S(1)}, u32[]{:S(2)}, u32[]{:S(2)}) %collective-permute-start.6) | collective-permute-done | bytes 1048608 | tf_op jit(solution)/shard_map/ppermute | solution.py:14
  294.9 2.1 collective-permute-start.7
  297.0 23.2 %collective-permute-done.7 = f32[512,512]{0,1:T(8,128)S(1)} collective-permute-done((f32[512,512]{0,1:T(8,128)S(1)}, f32[512,512]{0,1:T(8,128)S(1)}, u32[]{:S(2)}, u32[]{:S(2)}) %collective-permute-start.7) | collective-permute-done | bytes 1048608 | tf_op jit(solution)/shard_map/ppermute | solution.py:14
  320.4 2.8 collective-permute-start.8
  323.2 23.0 %collective-permute-done.8 = f32[512,512]{0,1:T(8,128)S(1)} collective-permute-done((f32[512,512]{0,1:T(8,128)S(1)}, f32[512,512]{0,1:T(8,128)S(1)}, u32[]{:S(2)}, u32[]{:S(2)}) %collective-permute-start.8) | collective-permute-done | bytes 1048608 | tf_op jit(solution)/shard_map/ppermute | solution.py:14
  1433.5 0.8 convolution_negate_fusion.127
  1434.3 0.9 convolution_negate_fusion.63
  1435.2 0.9 convolution_negate_fusion.31
  1436.1 0.9 convolution_negate_fusion.15
  1437.1 1.0 convolution_negate_fusion.7
  1438.1 1.0 convolution_negate_fusion.3
  1439.1 1.3 convolution_negate_fusion.1
  1440.4 1.4 convolution_negate_fusion
  1441.8 4.0 convolution_bitcast_fusion
  1446.0 3.0 copy.1518
  1455.1 0.8 fusion.2686
  1457.4 0.8 fusion.2695
  1458.1 0.8 fusion.2698
  1462.6 0.8 fusion.2716
  1464.8 0.8 fusion.2725
  1467.1 0.8 fusion.2734
  1468.6 0.8 fusion.2740
  1472.3 0.8 fusion.2755
  1474.5 0.8 fusion.2764
  1476.1 0.8 fusion.2770
  1480.6 0.8 fusion.2788
  1487.3 0.8 fusion.2815
  1491.8 0.8 fusion.2833
  1492.5 0.8 fusion.2836
  1496.3 0.8 fusion.1736
  1497.1 0.8 fusion.1741
  1500.2 0.8 fusion.1761
  1500.9 0.8 fusion.1766
  1502.5 0.8 fusion.1776
  1504.7 0.8 fusion.1791
  1505.5 0.8 fusion.1796
  1507.0 0.8 fusion.1806
  1513.0 0.8 fusion.1846
  1516.0 0.8 fusion.1866
  1516.7 0.8 fusion.1871
  1518.2 0.8 fusion.1881
  1522.8 0.8 fusion.1101
  1526.6 0.8 fusion.1136
  1533.4 0.8 fusion.663
  1534.2 0.8 fusion.672
  1538.8 0.8 fusion.390
  1540.4 0.8 fusion.217
  1541.2 0.8 fusion.230
  1542.1 4.9 fusion.63
  (2219 shorter events, 628.3 us)
Async XLA Ops:
  23.5 11.0 collective-permute-start
  34.7 27.2 %collective-permute-start.1 = (f32[512,512]{0,1:T(8,128)S(1)}, f32[512,512]{0,1:T(8,128)S(1)}, u32[]{:S(2)}, u32[]{:S(2)}) collective-permute-start(f32[512,512]{0,1:T(8,128)S(1)} %add.1047), channel_id=1, source_target_pairs={{0,2},{2,0},{1,3},{3,1},{4,6},{6,4},{5,7},{7,5},{8,10},{10,8},{9,1... | collective-permute-start | bytes 3145736 | tf_op jit(solution)/shard_map/ppermute | solution.py:14
  62.1 51.0 %collective-permute-start.2 = (f32[512,512]{0,1:T(8,128)S(1)}, f32[512,512]{0,1:T(8,128)S(1)}, u32[]{:S(2)}, u32[]{:S(2)}) collective-permute-start(f32[512,512]{0,1:T(8,128)S(1)} %add.1048), channel_id=1, source_target_pairs={{0,4},{4,0},{1,5},{5,1},{2,6},{6,2},{3,7},{7,3},{8,12},{12,8},{9,1... | collective-permute-start | bytes 3145736 | tf_op jit(solution)/shard_map/ppermute | solution.py:14
  113.4 52.9 %collective-permute-start.3 = (f32[512,512]{0,1:T(8,128)S(1)}, f32[512,512]{0,1:T(8,128)S(1)}, u32[]{:S(2)}, u32[]{:S(2)}) collective-permute-start(f32[512,512]{0,1:T(8,128)S(1)} %add.1049), channel_id=1, source_target_pairs={{0,8},{8,0},{1,9},{9,1},{2,10},{10,2},{3,11},{11,3},{4,12},{12,4},... | collective-permute-start | bytes 3145736 | tf_op jit(solution)/shard_map/ppermute | solution.py:14
  166.5 24.4 %collective-permute-start.4 = (f32[512,512]{0,1:T(8,128)S(1)}, f32[512,512]{0,1:T(8,128)S(1)}, u32[]{:S(2)}, u32[]{:S(2)}) collective-permute-start(f32[512,512]{0,1:T(8,128)S(1)} %add.1050), channel_id=1, source_target_pairs={{0,16},{16,0},{1,17},{17,1},{2,18},{18,2},{3,19},{19,3},{4,20},{20... | collective-permute-start | bytes 3145736 | tf_op jit(solution)/shard_map/ppermute | solution.py:14
  191.1 49.3 %collective-permute-start.5 = (f32[512,512]{0,1:T(8,128)S(1)}, f32[512,512]{0,1:T(8,128)S(1)}, u32[]{:S(2)}, u32[]{:S(2)}) collective-permute-start(f32[512,512]{0,1:T(8,128)S(1)} %add.1051), channel_id=1, source_target_pairs={{0,32},{32,0},{1,33},{33,1},{2,34},{34,2},{3,35},{35,3},{4,36},{36... | collective-permute-start | bytes 3145736 | tf_op jit(solution)/shard_map/ppermute | solution.py:14
  240.5 54.2 %collective-permute-start.6 = (f32[512,512]{0,1:T(8,128)S(1)}, f32[512,512]{0,1:T(8,128)S(1)}, u32[]{:S(2)}, u32[]{:S(2)}) collective-permute-start(f32[512,512]{0,1:T(8,128)S(1)} %add.1052), channel_id=1, source_target_pairs={{0,64},{64,0},{1,65},{65,1},{2,66},{66,2},{3,67},{67,3},{4,68},{68... | collective-permute-start | bytes 3145736 | tf_op jit(solution)/shard_map/ppermute | solution.py:14
  294.9 25.2 %collective-permute-start.7 = (f32[512,512]{0,1:T(8,128)S(1)}, f32[512,512]{0,1:T(8,128)S(1)}, u32[]{:S(2)}, u32[]{:S(2)}) collective-permute-start(f32[512,512]{0,1:T(8,128)S(1)} %add.1053), channel_id=1, source_target_pairs={{0,128},{128,0},{1,129},{129,1},{2,130},{130,2},{3,131},{131,3},{4... | collective-permute-start | bytes 3145736 | tf_op jit(solution)/shard_map/ppermute | solution.py:14
  320.4 25.8 %collective-permute-start.8 = (f32[512,512]{0,1:T(8,128)S(1)}, f32[512,512]{0,1:T(8,128)S(1)}, u32[]{:S(2)}, u32[]{:S(2)}) collective-permute-start(f32[512,512]{0,1:T(8,128)S(1)} %add.1054), channel_id=1, source_target_pairs={{0,256},{256,0},{1,257},{257,1},{2,258},{258,2},{3,259},{259,3},{4... | collective-permute-start | bytes 3145736 | tf_op jit(solution)/shard_map/ppermute | solution.py:14
  1437.1 4.7 copy-start.41
  1437.1 4.7 copy-start.42
  1445.7 74.0 %copy-start.19 = (f32[8,8]{0,1:T(8,128)S(1)}, f32[8,8]{0,1:T(8,128)}, u32[]{:S(2)}) copy-start(f32[8,8]{0,1:T(8,128)} %get-tuple-element.777) | copy-start | bytes 772
  1445.7 74.0 %copy-start.20 = (f32[8,8]{0,1:T(8,128)S(1)}, f32[8,8]{0,1:T(8,128)}, u32[]{:S(2)}) copy-start(f32[8,8]{0,1:T(8,128)} %copy.1272) | copy-start | bytes 772
  1445.7 74.0 %copy-start.30 = (f32[4,4]{0,1:T(4,128)S(1)}, f32[4,4]{0,1:T(4,128)}, u32[]{:S(2)}) copy-start(f32[4,4]{0,1:T(4,128)} %copy.1271) | copy-start | bytes 196
  1445.7 74.8 %copy-start.21 = (f32[8,8]{0,1:T(8,128)S(1)}, f32[8,8]{0,1:T(8,128)}, u32[]{:S(2)}) copy-start(f32[8,8]{0,1:T(8,128)} %copy.1287) | copy-start | bytes 772
  1445.8 74.8 %copy-start.32 = (f32[4,4]{0,1:T(4,128)S(1)}, f32[4,4]{0,1:T(4,128)}, u32[]{:S(2)}) copy-start(f32[4,4]{0,1:T(4,128)} %copy.1286) | copy-start | bytes 196
  1445.8 75.5 %copy-start.22 = (f32[8,8]{0,1:T(8,128)S(1)}, f32[8,8]{0,1:T(8,128)}, u32[]{:S(2)}) copy-start(f32[8,8]{0,1:T(8,128)} %copy.1303) | copy-start | bytes 772
  1445.8 75.5 %copy-start.34 = (f32[4,4]{0,1:T(4,128)S(1)}, f32[4,4]{0,1:T(4,128)}, u32[]{:S(2)}) copy-start(f32[4,4]{0,1:T(4,128)} %copy.1302) | copy-start | bytes 196
  1445.8 76.3 %copy-start.23 = (f32[8,8]{0,1:T(8,128)S(1)}, f32[8,8]{0,1:T(8,128)}, u32[]{:S(2)}) copy-start(f32[8,8]{0,1:T(8,128)} %copy.1318) | copy-start | bytes 772
  1445.8 76.3 %copy-start.36 = (f32[4,4]{0,1:T(4,128)S(1)}, f32[4,4]{0,1:T(4,128)}, u32[]{:S(2)}) copy-start(f32[4,4]{0,1:T(4,128)} %copy.1317) | copy-start | bytes 196
  1445.8 77.0 %copy-start.24 = (f32[8,8]{0,1:T(8,128)S(1)}, f32[8,8]{0,1:T(8,128)}, u32[]{:S(2)}) copy-start(f32[8,8]{0,1:T(8,128)} %copy.1335) | copy-start | bytes 772
  1445.8 77.0 %copy-start.37 = (f32[4,4]{0,1:T(4,128)S(1)}, f32[4,4]{0,1:T(4,128)}, u32[]{:S(2)}) copy-start(f32[4,4]{0,1:T(4,128)} %copy.1334) | copy-start | bytes 196
  1445.8 77.8 %copy-start.25 = (f32[8,8]{0,1:T(8,128)S(1)}, f32[8,8]{0,1:T(8,128)}, u32[]{:S(2)}) copy-start(f32[8,8]{0,1:T(8,128)} %copy.1350) | copy-start | bytes 772
  1445.8 77.8 %copy-start.39 = (f32[4,4]{0,1:T(4,128)S(1)}, f32[4,4]{0,1:T(4,128)}, u32[]{:S(2)}) copy-start(f32[4,4]{0,1:T(4,128)} %copy.1349) | copy-start | bytes 196
  1445.8 78.5 %copy-start.26 = (f32[8,8]{0,1:T(8,128)S(1)}, f32[8,8]{0,1:T(8,128)}, u32[]{:S(2)}) copy-start(f32[8,8]{0,1:T(8,128)} %copy.1366) | copy-start | bytes 772
  1445.9 79.3 %copy-start.27 = (f32[8,8]{0,1:T(8,128)S(1)}, f32[8,8]{0,1:T(8,128)}, u32[]{:S(2)}) copy-start(f32[8,8]{0,1:T(8,128)} %copy.1381) | copy-start | bytes 772
  1445.9 86.0 %copy-start.7 = (f32[16,16]{0,1:T(8,128)S(1)}, f32[16,16]{0,1:T(8,128)}, u32[]{:S(2)}) copy-start(f32[16,16]{0,1:T(8,128)} %copy.1280) | copy-start | bytes 3076
  1445.9 86.0 %copy-start.12 = (f32[8,8]{0,1:T(8,128)S(1)}, f32[8,8]{0,1:T(8,128)}, u32[]{:S(2)}) copy-start(f32[8,8]{0,1:T(8,128)} %copy.1279) | copy-start | bytes 772
  1445.9 86.0 %copy-start.31 = (f32[4,4]{0,1:T(4,128)S(1)}, f32[4,4]{0,1:T(4,128)}, u32[]{:S(2)}) copy-start(f32[4,4]{0,1:T(4,128)} %copy.1278) | copy-start | bytes 196
  1445.9 86.7 %copy-start.8 = (f32[16,16]{0,1:T(8,128)S(1)}, f32[16,16]{0,1:T(8,128)}, u32[]{:S(2)}) copy-start(f32[16,16]{0,1:T(8,128)} %copy.1311) | copy-start | bytes 3076
  1445.9 86.7 %copy-start.14 = (f32[8,8]{0,1:T(8,128)S(1)}, f32[8,8]{0,1:T(8,128)}, u32[]{:S(2)}) copy-start(f32[8,8]{0,1:T(8,128)} %copy.1310) | copy-start | bytes 772
  1445.9 86.7 %copy-start.35 = (f32[4,4]{0,1:T(4,128)S(1)}, f32[4,4]{0,1:T(4,128)}, u32[]{:S(2)}) copy-start(f32[4,4]{0,1:T(4,128)} %copy.1309) | copy-start | bytes 196
  1445.9 87.4 %copy-start.9 = (f32[16,16]{0,1:T(8,128)S(1)}, f32[16,16]{0,1:T(8,128)}, u32[]{:S(2)}) copy-start(f32[16,16]{0,1:T(8,128)} %copy.1343) | copy-start | bytes 3076
  1445.9 87.4 %copy-start.16 = (f32[8,8]{0,1:T(8,128)S(1)}, f32[8,8]{0,1:T(8,128)}, u32[]{:S(2)}) copy-start(f32[8,8]{0,1:T(8,128)} %copy.1342) | copy-start | bytes 772
  1445.9 87.4 %copy-start.38 = (f32[4,4]{0,1:T(4,128)S(1)}, f32[4,4]{0,1:T(4,128)}, u32[]{:S(2)}) copy-start(f32[4,4]{0,1:T(4,128)} %copy.1341) | copy-start | bytes 196
  1446.0 88.2 %copy-start.10 = (f32[16,16]{0,1:T(8,128)S(1)}, f32[16,16]{0,1:T(8,128)}, u32[]{:S(2)}) copy-start(f32[16,16]{0,1:T(8,128)} %copy.1374) | copy-start | bytes 3076
  1446.0 88.2 %copy-start.18 = (f32[8,8]{0,1:T(8,128)S(1)}, f32[8,8]{0,1:T(8,128)}, u32[]{:S(2)}) copy-start(f32[8,8]{0,1:T(8,128)} %copy.1373) | copy-start | bytes 772
  1449.0 88.9 %copy-start.1 = (f32[32,32]{0,1:T(8,128)S(1)}, f32[32,32]{0,1:T(8,128)}, u32[]{:S(2)}) copy-start(f32[32,32]{0,1:T(8,128)} %copy.1296) | copy-start | bytes 12292
  1449.0 88.9 %copy-start.4 = (f32[16,16]{0,1:T(8,128)S(1)}, f32[16,16]{0,1:T(8,128)}, u32[]{:S(2)}) copy-start(f32[16,16]{0,1:T(8,128)} %copy.1295) | copy-start | bytes 3076
  1449.0 88.9 %copy-start.13 = (f32[8,8]{0,1:T(8,128)S(1)}, f32[8,8]{0,1:T(8,128)}, u32[]{:S(2)}) copy-start(f32[8,8]{0,1:T(8,128)} %copy.1294) | copy-start | bytes 772
  1449.0 89.0 %copy-start.33 = (f32[4,4]{0,1:T(4,128)S(1)}, f32[4,4]{0,1:T(4,128)}, u32[]{:S(2)}) copy-start(f32[4,4]{0,1:T(4,128)} %copy.1293) | copy-start | bytes 196
  1449.0 89.7 %copy-start.2 = (f32[32,32]{0,1:T(8,128)S(1)}, f32[32,32]{0,1:T(8,128)}, u32[]{:S(2)}) copy-start(f32[32,32]{0,1:T(8,128)} %copy.1359) | copy-start | bytes 12292
  1449.0 89.7 %copy-start.6 = (f32[16,16]{0,1:T(8,128)S(1)}, f32[16,16]{0,1:T(8,128)}, u32[]{:S(2)}) copy-start(f32[16,16]{0,1:T(8,128)} %copy.1358) | copy-start | bytes 3076
  1449.0 89.7 %copy-start.17 = (f32[8,8]{0,1:T(8,128)S(1)}, f32[8,8]{0,1:T(8,128)}, u32[]{:S(2)}) copy-start(f32[8,8]{0,1:T(8,128)} %copy.1357) | copy-start | bytes 772
  1449.0 91.3 %copy-start.5 = (f32[16,16]{0,1:T(8,128)S(1)}, f32[16,16]{0,1:T(8,128)}, u32[]{:S(2)}) copy-start(f32[16,16]{0,1:T(8,128)} %copy.1326) | copy-start | bytes 3076
  1449.0 91.3 %copy-start.15 = (f32[8,8]{0,1:T(8,128)S(1)}, f32[8,8]{0,1:T(8,128)}, u32[]{:S(2)}) copy-start(f32[8,8]{0,1:T(8,128)} %copy.1325) | copy-start | bytes 772
  1449.1 91.3 %copy-start.28 = (f32[4,4]{0,1:T(4,128)S(1)}, f32[4,4]{0,1:T(4,128)}, u32[]{:S(2)}) copy-start(f32[4,4]{0,1:T(4,128)} %copy.1324) | copy-start | bytes 196
  1449.1 92.9 %copy-start = (f32[32,32]{0,1:T(8,128)S(1)}, f32[32,32]{0,1:T(8,128)}, u32[]{:S(2)}) copy-start(f32[32,32]{0,1:T(8,128)} %copy.1390) | copy-start | bytes 12292
  1449.1 92.9 %copy-start.3 = (f32[16,16]{0,1:T(8,128)S(1)}, f32[16,16]{0,1:T(8,128)}, u32[]{:S(2)}) copy-start(f32[16,16]{0,1:T(8,128)} %copy.1389) | copy-start | bytes 3076
  1449.1 92.9 %copy-start.11 = (f32[8,8]{0,1:T(8,128)S(1)}, f32[8,8]{0,1:T(8,128)}, u32[]{:S(2)}) copy-start(f32[8,8]{0,1:T(8,128)} %copy.1388) | copy-start | bytes 772
  1449.1 92.9 %copy-start.29 = (f32[4,4]{0,1:T(4,128)S(1)}, f32[4,4]{0,1:T(4,128)}, u32[]{:S(2)}) copy-start(f32[4,4]{0,1:T(4,128)} %copy.1387) | copy-start | bytes 196
  1520.5 21.4 %copy-start.40 = (f32[2,2]{0,1:T(2,128)S(1)}, f32[2,2]{0,1:T(2,128)}, u32[]{:S(2)}) copy-start(f32[2,2]{0,1:T(2,128)} %copy.1386) | copy-start | bytes 52
where the time goes:
time: 1560 us; the launch traced here: 1550 us
  between operations  530 us (34%)
  local copies, waits for them, and re-layouts  309 us (20%)
  waiting for transfers between devices  274 us (18%)
  matrix products  196 us (13%)
  other arithmetic  172 us (11%)
  starting transfers between devices  47.2 us (3%)
  blocking collectives  19.7 us (1%)
    ppermute x9, waiting for transfers between devices, partner(): return lax.ppermute(block, axis, route)  274 us
    dot_general x1021, matrix products, matmul(): jnp.dot(left, right, precision=lax.Precision.HIGHEST, preferred_element_t...  193 us
    slice x256, local copies, waits for them, and re-layouts, factor_pair(): lower_top, inv_top = factor_pair(matrix[:half, :half])  175 us
    concatenate x254, other arithmetic, factor_pair(): jnp.concatenate([jnp.concatenate([lower_top, zeros_top], axis=1), jnp.con...  143 us
    dot_general x252, local copies, waits for them, and re-layouts, matmul(): jnp.dot(left, right, precision=lax.Precision.HIGHEST, preferred_element_t...  129 us
    ppermute x9, starting transfers between devices, partner(): return lax.ppermute(block, axis, route)  47.2 us
  transfers between devices with their start and end apart: 9, of which 9 were waited for; matrix products, arithmetic and copies ran while one was open for 0% of the time, Pallas kernels for 0%

commit v1 on v0

v1 whole, which is shorter than its diff:
```python
import functools

import jax
import jax.numpy as jnp
from jax import lax
from jax.experimental import pallas as pl
from jax.experimental.pallas import tpu as pltpu
from jax.sharding import Mesh
from jax.sharding import PartitionSpec as P

B = 128
N = 512
STEPS = N // B
PAIRS = [(k, j) for k in range(STEPS) for j in range(k, STEPS)]
HALF = len(PAIRS) // 2
F32 = jnp.float32
SMEM = pl.BlockSpec(memory_space=pltpu.SMEM)
VMEM = pl.BlockSpec(memory_space=pltpu.VMEM)


def dot(left, right, left_dim=1, right_dim=0):
    return lax.dot_general(
        left,
        right,
        (((left_dim,), (right_dim,)), ((), ())),
        precision=lax.Precision.HIGHEST,
        preferred_element_type=F32,
    )


def factor_block(rows):
    count = len(rows)
    rows = list(rows)
    lane = lax.broadcasted_iota(jnp.int32, (8, B), 1)
    sub = lax.broadcasted_iota(jnp.int32, (8, B), 0)

    def spread(v):
        return jnp.broadcast_to(v, (8, B))

    upper, inverse = [], []
    for p in range(count):
        c0 = 8 * p
        cols = {q: [spread(rows[q][:, c0 + s : c0 + s + 1]) for s in range(8)] for q in range(p, count)}
        inside = (lane >= c0) & (lane < c0 + 8)
        rows[p] = jnp.where(inside, jnp.where(lane - c0 == sub, 1.0, 0.0), rows[p])
        for q in range(p + 1, count):
            rows[q] = jnp.where(inside, 0.0, rows[q])
        pivots = jnp.zeros((8, B), F32)
        for s in range(8):
            pivot = spread(cols[p][s][s : s + 1])
            pivots = jnp.where(sub == s, pivot, pivots)
            scale = 1.0 / pivot
            ahead = [spread(cols[p][t][s : s + 1]) if t > s else None for t in range(8)]
            row = spread(rows[p][s : s + 1])
            for q in range(p, count):
                factor = cols[q][s] * scale
                if q == p:
                    factor = jnp.where(sub > s, factor, 0.0)
                for t in range(s + 1, 8):
                    cols[q][t] = cols[q][t] - factor * ahead[t]
                rows[q] = rows[q] - factor * row
        root = lax.rsqrt(pivots)
        root = root * (1.5 - 0.5 * pivots * root * root)
        u = rows[p]
        for t in range(8):
            u = jnp.where(lane == c0 + t, cols[p][t], u)
        upper.append(jnp.where(lane >= c0 + sub, u, 0.0) * root)
        inverse.append(jnp.where(lane <= c0 + sub, rows[p], 0.0) * root)
    return jnp.concatenate(upper, 0), jnp.concatenate(inverse, 0)


def gram_kernel(scale, core, x, mine, theirs, parts):
    for k in range(STEPS):
        for j in range(k, STEPS):
            parts[PAIRS.index((k, j))] = dot(x[k], x[j], 0, 0) * scale
    mine[...] = parts[pl.ds(core[0] * HALF, HALF)].reshape(HALF * B, B)
    theirs[...] = parts[pl.ds((1 - core[0]) * HALF, HALF)].reshape(HALF * B, B)


def gram(core, x, scale):
    return pl.pallas_call(
        functools.partial(gram_kernel, scale),
        in_specs=[SMEM, VMEM],
        out_shape=[jax.ShapeDtypeStruct((HALF * B, B), F32)] * 2,
        scratch_shapes=[pltpu.VMEM((len(PAIRS), B, B), F32)],
        compiler_params=pltpu.CompilerParams(vmem_limit_bytes=32 << 20),
        name="gram",
    )(core, x)


def factor_kernel(core, mine, theirs, x, basis_ref, u_ref, m):
    for k in range(STEPS):
        for j in range(STEPS):
            here = (slice(k * B, k * B + B), slice(j * B, j * B + B))
            if j >= k:
                owner, at = divmod(PAIRS.index((k, j)), HALF)
                rows = slice(at * B, at * B + B)
                m[here] = jnp.where(core[0] == owner, mine[rows, :], theirs[rows, :])
            else:
                m[here] = jnp.zeros((B, B), F32)
    block = lax.broadcasted_iota(jnp.int32, (B, N), 1) // B

    @pl.loop(0, STEPS)
    def _(k):
        o = pl.multiple_of(k * B, B)
        here = pl.ds(o, B)
        uk, ik = factor_block([m[pl.ds(o + 8 * q, 8), here] for q in range(B // 8)])
        panel = dot(ik, m[here, :])
        m[here, :] = panel
        m[here, here] = ik
        u_ref[here, :] = jnp.where(block > k, panel, 0.0)
        u_ref[here, here] = uk
        for i in range(1, STEPS):
            rows = slice(i * B, i * B + B)

            @pl.when(i > k)
            def _():
                m[rows, :] = jnp.where(block == k, 0.0, m[rows, :]) - dot(u_ref[here, rows], m[here, :], 0, 0)

    for j in range(STEPS):
        total = dot(x[0], m[j * B : j * B + B, :B], 1, 1)
        for g in range(1, j + 1):
            total = total + dot(x[g], m[j * B : j * B + B, g * B : g * B + B], 1, 1)
        basis_ref[:, j * B : j * B + B] = total


def factor(core, mine, theirs, x):
    return pl.pallas_call(
        factor_kernel,
        in_specs=[SMEM, VMEM, VMEM, VMEM],
        out_shape=[jax.ShapeDtypeStruct((x.shape[1], N), F32), jax.ShapeDtypeStruct((N, N), F32)],
        scratch_shapes=[pltpu.VMEM((N, N), F32)],
        compiler_params=pltpu.CompilerParams(vmem_limit_bytes=32 << 20),
        name="factor",
    )(core, mine, theirs, x)


def other_core(v):
    return lax.ppermute(v, "core", [(0, 1), (1, 0)])


def from_x(v, d):
    count = lax.axis_size("x")
    return lax.ppermute(v, "x", [(i, (i + d) % count) for i in range(count)])


def all_sum(mine, theirs):
    mine = mine + other_core(theirs)
    rows = mine.shape[0]
    peers = lax.axis_size(("y", "z"))
    pieces = mine.reshape(peers, rows // peers, B)
    pieces = lax.all_to_all(pieces, ("y", "z"), split_axis=0, concat_axis=0, tiled=True)
    piece = jnp.sum(pieces, axis=0)
    total = (piece + from_x(piece, 2)) + (from_x(piece, 1) + from_x(piece, 3))
    pieces = jnp.broadcast_to(total[None], (peers,) + total.shape)
    pieces = lax.all_to_all(pieces, ("y", "z"), split_axis=0, concat_axis=0, tiled=True)
    mine = pieces.reshape(rows, B)
    return mine, other_core(mine)


def local(sketch):
    groups = lax.axis_size("x")
    x = lax.all_to_all(sketch.reshape(groups, -1, B), "x", split_axis=0, concat_axis=0, tiled=True)
    total_rows = x.shape[1] * lax.axis_size(("x", "y", "z", "core"))
    core = lax.axis_index("core").reshape(1)
    mine, theirs = gram(core, x, 1.0 / total_rows)
    mine, theirs = all_sum(mine, theirs)
    return factor(core, mine, theirs, x)


def solution(mesh):
    grp, row = mesh.devices.shape
    core = 2
    side = 8
    grid = Mesh(mesh.devices.reshape(grp, row // (side * core), side, core), ("x", "y", "z", "core"))
    row_axes = ("y", "z", "core")
    return jax.shard_map(
        local,
        mesh=grid,
        in_specs=(P(row_axes, "x"),),
        out_specs=(P(row_axes + ("x",), None), P()),
        check_vma=False,
    )
```

time: 1560 us -> 135 us (0.09)
  between operations: 530 us -> 0.71 us
  local copies, waits for them, and re-layouts: 309 us -> 0.11 us
  waiting for transfers between devices: 274 us -> 20.5 us
  matrix products: 196 us -> 0 us
  other arithmetic: 172 us -> 0.13 us
  blocking collectives: 19.7 us -> 55 us
  Pallas kernels: 0 us -> 28.4 us
  starting transfers between devices: 47.2 us -> 29.3 us
    ppermute x9 -> x5, waiting for transfers between devices: 274 us -> 5.64 us  [the longest x3 3.36 us: from_x(): return lax.ppermute(v, 'x', [(i, (i + d) % count) for i in range(count)])]
    dot_general x1022 -> x0, matrix products: 196 us -> none  [the longest x1021 193 us: matmul(): jnp.dot(left, right, precision=lax.Precision.HIGHEST, preferred_element_t...]
    slice x256 -> x0, local copies, waits for them, and re-layouts: 175 us -> none  [factor_pair(): lower_top, inv_top = factor_pair(matrix[:half, :half])]
    concatenate x509 -> x0, other arithmetic: 165 us -> none  [the longest x254 143 us: factor_pair(): jnp.concatenate([jnp.concatenate([lower_top, zeros_top], axis=1), jnp.con...]
    dot_general x252 -> x0, local copies, waits for them, and re-layouts: 129 us -> none  [matmul(): jnp.dot(left, right, precision=lax.Precision.HIGHEST, preferred_element_t...]
    all_to_all x1 -> x2, blocking collectives: 19.7 us -> 55 us  [all_sum(): lax.all_to_all(pieces, ('y', 'z'), split_axis=0, concat_axis=0, tiled=True)]
    pallas_call x0 -> x2, Pallas kernels: none -> 28.4 us  [the longest x1 24.9 us: factor(): pl.pallas_call(factor_kernel, in_specs=[SMEM, VMEM, VMEM, VMEM], out_shap...]
    ppermute x9 -> x5, starting transfers between devices: 47.2 us -> 24.4 us  [the longest x2 16.6 us: other_core(): return lax.ppermute(v, 'core', [(0, 1), (1, 0)])]
  transfers between devices with their start and end apart: 9 -> 6, of which waited for: 9 -> 5; matrix products, arithmetic and copies ran while one was open for 0% -> 0% of each run, Pallas kernels for 0% -> 0%
where the time goes in v1:
time: 135 us; the launch traced here: 134 us
  blocking collectives  55 us (41%)
  starting transfers between devices  29.3 us (22%)
  Pallas kernels  28.4 us (21%)
  waiting for transfers between devices  20.5 us (15%)
    all_to_all x2, blocking collectives, all_sum(): lax.all_to_all(pieces, ('y', 'z'), split_axis=0, concat_axis=0, tiled=True)  55 us
    pallas_call x1, Pallas kernels, factor(): pl.pallas_call(factor_kernel, in_specs=[SMEM, VMEM, VMEM, VMEM], out_shap...  24.9 us
    ppermute x2, starting transfers between devices, other_core(): return lax.ppermute(v, 'core', [(0, 1), (1, 0)])  16.6 us
    all_to_all x1, waiting for transfers between devices, local(): lax.all_to_all(sketch.reshape(groups, -1, B), 'x', split_axis=0, concat_a...  14.9 us
    ppermute x3, starting transfers between devices, from_x(): return lax.ppermute(v, 'x', [(i, (i + d) % count) for i in range(count)])  7.8 us
    all_to_all x1, starting transfers between devices, local(): lax.all_to_all(sketch.reshape(groups, -1, B), 'x', split_axis=0, concat_a...  4.85 us
    pallas_call x1, Pallas kernels, gram(): pl.pallas_call(functools.partial(gram_kernel, scale), in_specs=[SMEM, VME...  3.55 us
    ppermute x3, waiting for transfers between devices, from_x(): return lax.ppermute(v, 'x', [(i, (i + d) % count) for i in range(count)])  3.36 us
  transfers between devices with their start and end apart: 6, of which 5 were waited for; matrix products, arithmetic and copies ran while one was open for 0% of the time, Pallas kernels for 0%

profile of v1, /device:TPU:1, one launch (start us, length us, event | category | flops | bytes accessed | tf_op | source)
XLA Modules:
  0.0 134.1 jit_solution(7956126274002349586)
XLA Ops:
  0.6 4.9 %all-to-all-start = ((f32[4,768,128]{2,1,0:T(8,128)}), f32[4,768,128]{2,1,0:T(8,128)S(1)}, u32[]{:S(2)}, u32[]{:S(2)}) async-start(f32[4,768,128]{2,1,0:T(8,128)} %bitcast.2), calls=%async_computation | async-start | bytes 3145728 | tf_op jit(solution)/shard_map/all_to_all | solution.py:163
  5.5 14.9 %all-to-all-done.x = f32[4,768,128]{2,1,0:T(8,128)S(1)} async-done(((f32[4,768,128]{2,1,0:T(8,128)}), f32[4,768,128]{2,1,0:T(8,128)S(1)}, u32[]{:S(2)}, u32[]{:S(2)}) %all-to-all-start) | async-done | bytes 1572896 | tf_op jit(solution)/shard_map/all_to_all | solution.py:163
  20.4 3.5 %gram.1 = (f32[640,128]{1,0:T(8,128)S(1)}, f32[640,128]{1,0:T(8,128)S(1)}) custom-call(s32[1]{0:T(128)} %bitcast.core, f32[4,768,128]{2,1,0:T(8,128)S(1)} %all-to-all-done.x), custom_call_target="tpu_custom_call" | custom-call | tf_op jit(solution)/shard_map/gram/pallas_call | solution.py:81
  23.9 8.7 %collective-permute-start = (f32[640,128]{1,0:T(8,128)S(1)}, f32[640,128]{1,0:T(8,128)S(1)}, u32[]{:S(2)}, u32[]{:S(2)}) collective-permute-start(f32[640,128]{1,0:T(8,128)S(1)} %get-tuple-element.5), channel_id=1, source_target_pairs={{0,1},{1,0},{2,3},{3,2},{4,5},{5,4},{6,7},{7,6},{8,9},{9,8},{10,11... | collective-permute-start | bytes 983048 | tf_op jit(solution)/shard_map/ppermute | solution.py:139
  32.6 1.2 collective-permute-done
  33.9 32.8 %all_to_all.15 = f32[64,10,128]{2,1,0:T(8,128)S(1)} all-to-all(f32[64,10,128]{2,1,0:T(8,128)S(1)} %reshape.19), channel_id=1, replica_groups=mesh['x'=4,'y'=8,'z'=8,'core'=2] {'y','z'}, dimensions={0} | all-to-all | bytes 655360 | tf_op jit(solution)/shard_map/all_to_all | solution.py:152
  66.8 0.1 reduce_sum.9
  66.8 2.8 %collective-permute-start.3 = (f32[10,128]{1,0:T(8,128)S(1)}, f32[10,128]{1,0:T(8,128)S(1)}, u32[]{:S(2)}, u32[]{:S(2)}) collective-permute-start(f32[10,128]{1,0:T(8,128)S(1)} %reduce_sum.9), channel_id=1, source_target_pairs={{0,384},{128,0},{256,128},{384,256},{1,385},{129,1},{257,129},{385... | collective-permute-start | bytes 15368 | tf_op jit(solution)/shard_map/ppermute | solution.py:144
  69.6 2.5 %collective-permute-start.2 = (f32[10,128]{1,0:T(8,128)S(1)}, f32[10,128]{1,0:T(8,128)S(1)}, u32[]{:S(2)}, u32[]{:S(2)}) collective-permute-start(f32[10,128]{1,0:T(8,128)S(1)} %reduce_sum.9), channel_id=1, source_target_pairs={{0,128},{128,256},{256,384},{384,0},{1,129},{129,257},{257,385},{3... | collective-permute-start | bytes 15368 | tf_op jit(solution)/shard_map/ppermute | solution.py:144
  72.1 2.5 %collective-permute-start.1 = (f32[10,128]{1,0:T(8,128)S(1)}, f32[10,128]{1,0:T(8,128)S(1)}, u32[]{:S(2)}, u32[]{:S(2)}) collective-permute-start(f32[10,128]{1,0:T(8,128)S(1)} %reduce_sum.9), channel_id=1, source_target_pairs={{0,256},{128,384},{256,0},{384,128},{1,257},{129,385},{257,1},{385... | collective-permute-start | bytes 15368 | tf_op jit(solution)/shard_map/ppermute | solution.py:144
  74.7 0.0 collective-permute-done.3
  74.7 0.6 collective-permute-done.2
  75.2 2.8 %collective-permute-done.1 = f32[10,128]{1,0:T(8,128)S(1)} collective-permute-done((f32[10,128]{1,0:T(8,128)S(1)}, f32[10,128]{1,0:T(8,128)S(1)}, u32[]{:S(2)}, u32[]{:S(2)}) %collective-permute-start.1) | collective-permute-done | bytes 5152 | tf_op jit(solution)/shard_map/ppermute | solution.py:144
  78.1 22.2 %all_to_all.16 = f32[64,10,128]{2,1,0:T(8,128)S(1)} all-to-all(f32[64,10,128]{2,1,0:T(8,128)S(1)} %broadcast_in_dim.2), channel_id=1, replica_groups=mesh['x'=4,'y'=8,'z'=8,'core'=2] {'y','z'}, dimensions={0} | all-to-all | bytes 655360 | tf_op jit(solution)/shard_map/all_to_all | solution.py:156
  100.3 7.9 %collective-permute-start.4 = (f32[640,128]{1,0:T(8,128)S(1)}, f32[640,128]{1,0:T(8,128)S(1)}, u32[]{:S(2)}, u32[]{:S(2)}) collective-permute-start(f32[640,128]{1,0:T(8,128)S(1)} %reshape.20.mine), channel_id=1, source_target_pairs={{0,1},{1,0},{2,3},{3,2},{4,5},{5,4},{6,7},{7,6},{8,9},{9,8},{10,11... | collective-permute-start | bytes 983048 | tf_op jit(solution)/shard_map/ppermute | solution.py:139
  108.2 1.1 collective-permute-done.4.theirs
  109.3 24.9 %factor.1 = (f32[768,512]{1,0:T(8,128)}, f32[512,512]{1,0:T(8,128)}) custom-call(s32[1]{0:T(128)} %bitcast.core, f32[640,128]{1,0:T(8,128)S(1)} %reshape.20.mine, f32[640,128]{1,0:T(8,128)S(1)} %collective-permute-done.4.theirs, f32[4,768,128]{2,1,0:T(8,128)S(1)} %all-to-all-done.x), custom_call_target="tpu_custom_call" | custom-call | tf_op jit(solution)/shard_map/factor/pallas_call | solution.py:128
  (5 shorter events, 0.2 us)
Async XLA Ops:
  0.6 19.7 %all-to-all-start = ((f32[4,768,128]{2,1,0:T(8,128)}), f32[4,768,128]{2,1,0:T(8,128)S(1)}, u32[]{:S(2)}, u32[]{:S(2)}) async-start(f32[4,768,128]{2,1,0:T(8,128)} %bitcast.2), calls=%async_computation | async-start | bytes 3145728 | tf_op jit(solution)/shard_map/all_to_all | solution.py:163
  23.9 9.9 %collective-permute-start = (f32[640,128]{1,0:T(8,128)S(1)}, f32[640,128]{1,0:T(8,128)S(1)}, u32[]{:S(2)}, u32[]{:S(2)}) collective-permute-start(f32[640,128]{1,0:T(8,128)S(1)} %get-tuple-element.5), channel_id=1, source_target_pairs={{0,1},{1,0},{2,3},{3,2},{4,5},{5,4},{6,7},{7,6},{8,9},{9,8},{10,11... | collective-permute-start | bytes 983048 | tf_op jit(solution)/shard_map/ppermute | solution.py:139
  66.8 7.8 %collective-permute-start.3 = (f32[10,128]{1,0:T(8,128)S(1)}, f32[10,128]{1,0:T(8,128)S(1)}, u32[]{:S(2)}, u32[]{:S(2)}) collective-permute-start(f32[10,128]{1,0:T(8,128)S(1)} %reduce_sum.9), channel_id=1, source_target_pairs={{0,384},{128,0},{256,128},{384,256},{1,385},{129,1},{257,129},{385... | collective-permute-start | bytes 15368 | tf_op jit(solution)/shard_map/ppermute | solution.py:144
  69.6 5.6 %collective-permute-start.2 = (f32[10,128]{1,0:T(8,128)S(1)}, f32[10,128]{1,0:T(8,128)S(1)}, u32[]{:S(2)}, u32[]{:S(2)}) collective-permute-start(f32[10,128]{1,0:T(8,128)S(1)} %reduce_sum.9), channel_id=1, source_target_pairs={{0,128},{128,256},{256,384},{384,0},{1,129},{129,257},{257,385},{3... | collective-permute-start | bytes 15368 | tf_op jit(solution)/shard_map/ppermute | solution.py:144
  72.1 5.9 %collective-permute-start.1 = (f32[10,128]{1,0:T(8,128)S(1)}, f32[10,128]{1,0:T(8,128)S(1)}, u32[]{:S(2)}, u32[]{:S(2)}) collective-permute-start(f32[10,128]{1,0:T(8,128)S(1)} %reduce_sum.9), channel_id=1, source_target_pairs={{0,256},{128,384},{256,0},{384,128},{1,257},{129,385},{257,1},{385... | collective-permute-start | bytes 15368 | tf_op jit(solution)/shard_map/ppermute | solution.py:144
  100.3 9.0 %collective-permute-start.4 = (f32[640,128]{1,0:T(8,128)S(1)}, f32[640,128]{1,0:T(8,128)S(1)}, u32[]{:S(2)}, u32[]{:S(2)}) collective-permute-start(f32[640,128]{1,0:T(8,128)S(1)} %reshape.20.mine), channel_id=1, source_target_pairs={{0,1},{1,0},{2,3},{3,2},{4,5},{5,4},{6,7},{7,6},{8,9},{9,8},{10,11... | collective-permute-start | bytes 983048 | tf_op jit(solution)/shard_map/ppermute | solution.py:139

commit v2 on v1

v2 whole, which is shorter than its diff:
```python
import functools

import jax
import jax.numpy as jnp
from jax import lax
from jax.experimental import pallas as pl
from jax.experimental.pallas import tpu as pltpu
from jax.sharding import Mesh
from jax.sharding import PartitionSpec as P

B = 128
N = 512
STEPS = N // B
PAIRS = [(k, j) for k in range(STEPS) for j in range(k, STEPS)]
HALF = len(PAIRS) // 2
F32 = jnp.float32
BF16 = jnp.bfloat16
NEAR = 3
SMEM = pl.BlockSpec(memory_space=pltpu.SMEM)
VMEM = pl.BlockSpec(memory_space=pltpu.VMEM)


def dot(left, right, left_dim=1, right_dim=0):
    return lax.dot_general(
        left,
        right,
        (((left_dim,), (right_dim,)), ((), ())),
        precision=lax.Precision.HIGHEST,
        preferred_element_type=F32,
    )


def split(v):
    high = v.astype(BF16).astype(F32)
    rest = v - high
    middle = rest.astype(BF16).astype(F32)
    return high, middle, rest - middle


def wide_dot(left, right, left_dim, right_dim):
    a, b, c = split(left)
    d, e, f = split(right)
    left = jnp.concatenate([a, a, b, b, a, c], left_dim).astype(BF16)
    right = jnp.concatenate([d, e, d, e, f, d], right_dim).astype(BF16)
    return lax.dot_general(left, right, (((left_dim,), (right_dim,)), ((), ())), preferred_element_type=F32)


def factor_block(rows, after):
    count = len(rows)
    rows = list(rows)
    lane = lax.broadcasted_iota(jnp.int32, (8, B), 1)
    sub = lax.broadcasted_iota(jnp.int32, (8, B), 0)

    def spread(v):
        return jnp.broadcast_to(v, (8, B))

    def columns(q, first):
        return [spread(rows[q][:, first + s : first + s + 1]) for s in range(8)]

    upper, inverse = [], []
    coming = columns(0, 0)
    for p in range(count):
        c0 = 8 * p
        inside = (lane >= c0) & (lane < c0 + 8)
        cols = coming
        own = jnp.where(inside, jnp.where(lane - c0 == sub, 1.0, 0.0), rows[p])
        last = p + 1 == count
        below = None if last else columns(p + 1, c0)
        coming = None if last else columns(p + 1, c0 + 8)
        pivots = jnp.zeros((8, B), F32)
        scales, ahead, pivot_rows = [], [], []
        for s in range(8):
            pivot = spread(cols[s][s : s + 1])
            pivots = jnp.where(sub == s, pivot, pivots)
            scales.append(1.0 / pivot)
            ahead.append([spread(cols[t][s : s + 1]) if t > s else None for t in range(8)])
            pivot_rows.append(spread(own[s : s + 1]))
            factor = jnp.where(sub > s, cols[s], 0.0) * scales[s]
            for t in range(s + 1, 8):
                cols[t] = cols[t] - factor * ahead[s][t]
            own = own - factor * pivot_rows[s]
        for q in range(p + 1, min(count, p + 1 + NEAR)):
            here = below if q == p + 1 else columns(q, c0)
            target = jnp.where(inside, 0.0, rows[q])
            for s in range(8):
                factor = here[s] * scales[s]
                for t in range(s + 1, 8):
                    here[t] = here[t] - factor * ahead[s][t]
                if q == p + 1:
                    coming = [coming[t] - factor * spread(here[s][t : t + 1]) for t in range(8)]
                target = target - factor * pivot_rows[s]
            rows[q] = target
        root = lax.rsqrt(pivots)
        root = root * (1.5 - 0.5 * pivots * root * root)
        scaled = own * root
        far = p + 1 + NEAR
        if far < count:
            update = wide_dot(scaled, scaled, 0, 0)
            for q in range(far, count):
                rows[q] = jnp.where(inside, 0.0, rows[q]) - update[8 * q : 8 * q + 8]
        u = own
        for t in range(8):
            u = jnp.where(lane == c0 + t, cols[t], u)
        upper.append(jnp.where(lane >= c0 + sub, u, 0.0) * root)
        inverse.append(jnp.where(lane <= c0 + sub, scaled, 0.0))
        after(p)
    return jnp.concatenate(upper, 0), jnp.concatenate(inverse, 0)


def gram_kernel(scale, core, x, mine, theirs, parts):
    wide = [jnp.concatenate([x[2 * h], x[2 * h + 1]], 1) for h in range(2)]
    for h, i in ((0, 0), (0, 1), (1, 1)):
        product = dot(wide[h], wide[i], 0, 0) * scale
        for k in (2 * h, 2 * h + 1):
            for j in (2 * i, 2 * i + 1):
                if j >= k:
                    parts[PAIRS.index((k, j))] = product[k % 2 * B : k % 2 * B + B, j % 2 * B : j % 2 * B + B]
    mine[...] = parts[pl.ds(core[0] * HALF, HALF)].reshape(HALF * B, B)
    theirs[...] = parts[pl.ds((1 - core[0]) * HALF, HALF)].reshape(HALF * B, B)


def gram(core, x, scale):
    return pl.pallas_call(
        functools.partial(gram_kernel, scale),
        in_specs=[SMEM, VMEM],
        out_shape=[jax.ShapeDtypeStruct((HALF * B, B), F32)] * 2,
        scratch_shapes=[pltpu.VMEM((len(PAIRS), B, B), F32)],
        compiler_params=pltpu.CompilerParams(vmem_limit_bytes=32 << 20),
        name="gram",
    )(core, x)


def factor_kernel(core, mine, theirs, x, basis_ref, u_ref, m):
    todo = []

    def after(p):
        for _ in range(-(-len(todo) // (B // 8 - p))):
            todo.pop(0)()

    def block(k):
        return slice(k * B, k * B + B)

    def panel(k, j, inverse):
        r = wide_dot(inverse, m[block(k), block(j)], 1, 0)
        m[block(k), block(j)] = r
        if j > k:
            u_ref[block(k), block(j)] = r

    def trail(k, i, j):
        d = wide_dot(u_ref[block(k), block(i)], m[block(k), block(j)], 0, 0)
        m[block(i), block(j)] = -d if j == k else m[block(i), block(j)] - d

    def basis(h, rows):
        cols = slice(2 * h * B, 2 * h * B + 2 * B)
        m[block(2 * h), block(2 * h + 1)] = jnp.zeros((B, B), F32)
        left = jnp.concatenate([x[g, rows, :] for g in range(2 * h + 2)], 1)
        basis_ref[rows, cols] = dot(left, m[cols, : cols.stop], 1, 1)

    for k, j in PAIRS:
        owner, at = divmod(PAIRS.index((k, j)), HALF)
        m[block(k), block(j)] = jnp.where(core[0] == owner, mine[block(at), :], theirs[block(at), :])
    for k in range(STEPS):
        rows = [m[k * B + 8 * q : k * B + 8 * q + 8, block(k)] for q in range(B // 8)]
        upper, inverse = factor_block(rows, after)
        u_ref[block(k), block(k)] = upper
        for j in range(k):
            u_ref[block(k), block(j)] = jnp.zeros((B, B), F32)
        if k + 1 < STEPS:
            panel(k, k + 1, inverse)
            trail(k, k + 1, k + 1)
        m[block(k), block(k)] = inverse
        todo += [functools.partial(panel, k, j, inverse) for j in range(STEPS) if j not in (k, k + 1)]
        for i in range(k + 1, STEPS):
            for j in range(STEPS):
                if (j <= k or j >= i) and (i, j) != (k + 1, k + 1):
                    todo.append(functools.partial(trail, k, i, j))
        if k == STEPS // 2:
            todo += [functools.partial(basis, 0, slice(c, c + 2 * B)) for c in range(0, x.shape[1], 2 * B)]
    todo += [functools.partial(basis, 1, slice(0, x.shape[1]))]
    while todo:
        todo.pop(0)()


def factor(core, mine, theirs, x):
    return pl.pallas_call(
        factor_kernel,
        in_specs=[SMEM, VMEM, VMEM, VMEM],
        out_shape=[jax.ShapeDtypeStruct((x.shape[1], N), F32), jax.ShapeDtypeStruct((N, N), F32)],
        scratch_shapes=[pltpu.VMEM((N, N), F32)],
        compiler_params=pltpu.CompilerParams(vmem_limit_bytes=32 << 20),
        name="factor",
    )(core, mine, theirs, x)


def other_core(v):
    return lax.ppermute(v, "core", [(0, 1), (1, 0)])


def from_x(v, d):
    count = lax.axis_size("x")
    return lax.ppermute(v, "x", [(i, (i + d) % count) for i in range(count)])


def all_sum(mine, theirs):
    mine = mine + other_core(theirs)
    rows = mine.shape[0]
    peers = lax.axis_size(("y", "z"))
    pieces = mine.reshape(peers, rows // peers // 2, 2, B)
    pieces = lax.all_to_all(pieces, ("y", "z"), split_axis=0, concat_axis=0, tiled=True)
    piece = jnp.sum(pieces, axis=0)
    total = (piece + from_x(piece, 2)) + (from_x(piece, 1) + from_x(piece, 3))
    pieces = jnp.broadcast_to(total[None], (peers,) + total.shape)
    pieces = lax.all_to_all(pieces, ("y", "z"), split_axis=0, concat_axis=0, tiled=True)
    mine = pieces.reshape(rows, B)
    return mine, other_core(mine)


def local(sketch):
    groups = lax.axis_size("x")
    x = lax.all_to_all(sketch.reshape(groups, -1, B), "x", split_axis=0, concat_axis=0, tiled=True)
    total_rows = x.shape[1] * lax.axis_size(("x", "y", "z", "core"))
    core = lax.axis_index("core").reshape(1)
    mine, theirs = gram(core, x, 1.0 / total_rows)
    mine, theirs = all_sum(mine, theirs)
    return factor(core, mine, theirs, x)


def solution(mesh):
    grp, row = mesh.devices.shape
    core = 2
    side = 8
    grid = Mesh(mesh.devices.reshape(grp, row // (side * core), side, core), ("x", "y", "z", "core"))
    row_axes = ("y", "z", "core")
    return jax.shard_map(
        local,
        mesh=grid,
        in_specs=(P(row_axes, "x"),),
        out_specs=(P(row_axes + ("x",), None), P()),
        check_vma=False,
    )
```

time: 135 us -> 116 us (0.86)
  Pallas kernels: 28.4 us -> 17.6 us
  blocking collectives: 55 us -> 48.8 us
  starting transfers between devices: 29.3 us -> 27.7 us
    pallas_call x1, Pallas kernels: 24.9 us -> 15.4 us  [factor(): pl.pallas_call(factor_kernel, in_specs=[SMEM, VMEM, VMEM, VMEM], out_shap...]
    all_to_all x2, blocking collectives: 55 us -> 48.8 us  [all_sum(): lax.all_to_all(pieces, ('y', 'z'), split_axis=0, concat_axis=0, tiled=True)]
    ppermute x2, starting transfers between devices: 16.6 us -> 15.1 us  [other_core(): return lax.ppermute(v, 'core', [(0, 1), (1, 0)])]
    pallas_call x1, Pallas kernels: 3.55 us -> 2.17 us  [gram(): pl.pallas_call(functools.partial(gram_kernel, scale), in_specs=[SMEM, VME...]
where the time goes in v2:
time: 116 us
  blocking collectives  48.8 us (42%)
  starting transfers between devices  27.7 us (24%)
  waiting for transfers between devices  20.5 us (18%)
  Pallas kernels  17.6 us (15%)
    all_to_all x2, blocking collectives, all_sum(): lax.all_to_all(pieces, ('y', 'z'), split_axis=0, concat_axis=0, tiled=True)  48.8 us
    pallas_call x1, Pallas kernels, factor(): pl.pallas_call(factor_kernel, in_specs=[SMEM, VMEM, VMEM, VMEM], out_shap...  15.4 us
    ppermute x2, starting transfers between devices, other_core(): return lax.ppermute(v, 'core', [(0, 1), (1, 0)])  15.1 us
    all_to_all x1, waiting for transfers between devices, local(): lax.all_to_all(sketch.reshape(groups, -1, B), 'x', split_axis=0, concat_a...  14.9 us
    ppermute x3, starting transfers between devices, from_x(): return lax.ppermute(v, 'x', [(i, (i + d) % count) for i in range(count)])  7.8 us
    all_to_all x1, starting transfers between devices, local(): lax.all_to_all(sketch.reshape(groups, -1, B), 'x', split_axis=0, concat_a...  4.85 us
    ppermute x3, waiting for transfers between devices, from_x(): return lax.ppermute(v, 'x', [(i, (i + d) % count) for i in range(count)])  3.32 us
  transfers between devices with their start and end apart: 6, of which 5 were waited for; matrix products, arithmetic and copies ran while one was open for 0% of the time, Pallas kernels for 0%

profile of v2, /device:TPU:1, one launch (start us, length us, event | category | flops | bytes accessed | tf_op | source)
XLA Modules:
  0.0 115.6 jit_solution(10545444212722567333)
XLA Ops:
  0.6 4.9 %all-to-all-start = ((f32[4,768,128]{2,1,0:T(8,128)}), f32[4,768,128]{2,1,0:T(8,128)S(1)}, u32[]{:S(2)}, u32[]{:S(2)}) async-start(f32[4,768,128]{2,1,0:T(8,128)} %bitcast.6), calls=%async_computation | async-start | bytes 3145728 | tf_op jit(solution)/shard_map/all_to_all | solution.py:220
  5.5 14.9 %all-to-all-done.x = f32[4,768,128]{2,1,0:T(8,128)S(1)} async-done(((f32[4,768,128]{2,1,0:T(8,128)}), f32[4,768,128]{2,1,0:T(8,128)S(1)}, u32[]{:S(2)}, u32[]{:S(2)}) %all-to-all-start) | async-done | bytes 1572896 | tf_op jit(solution)/shard_map/all_to_all | solution.py:220
  20.4 2.2 %gram.1 = (f32[640,128]{1,0:T(8,128)S(1)}, f32[640,128]{1,0:T(8,128)S(1)}) custom-call(s32[1]{0:T(128)} %bitcast.core, f32[4,768,128]{2,1,0:T(8,128)S(1)} %all-to-all-done.x), custom_call_target="tpu_custom_call" | custom-call | tf_op jit(solution)/shard_map/gram/pallas_call | solution.py:123
  22.5 8.7 %collective-permute-start = (f32[640,128]{1,0:T(8,128)S(1)}, f32[640,128]{1,0:T(8,128)S(1)}, u32[]{:S(2)}, u32[]{:S(2)}) collective-permute-start(f32[640,128]{1,0:T(8,128)S(1)} %get-tuple-element.5), channel_id=1, source_target_pairs={{0,1},{1,0},{2,3},{3,2},{4,5},{5,4},{6,7},{7,6},{8,9},{9,8},{10,11... | collective-permute-start | bytes 983048 | tf_op jit(solution)/shard_map/ppermute | solution.py:196
  31.2 1.2 %collective-permute-done = f32[640,128]{1,0:T(8,128)S(1)} collective-permute-done((f32[640,128]{1,0:T(8,128)S(1)}, f32[640,128]{1,0:T(8,128)S(1)}, u32[]{:S(2)}, u32[]{:S(2)}) %collective-permute-start) | collective-permute-done | bytes 327712 | tf_op jit(solution)/shard_map/ppermute | solution.py:196
  32.5 30.2 %all_to_all.15 = f32[64,5,2,128]{3,2,1,0:T(2,128)S(1)} all-to-all(f32[64,5,2,128]{3,2,1,0:T(2,128)S(1)} %bitcast.7), channel_id=1, replica_groups=mesh['x'=4,'y'=8,'z'=8,'core'=2] {'y','z'}, dimensions={0} | all-to-all | bytes 655360 | tf_op jit(solution)/shard_map/all_to_all | solution.py:209
  62.7 0.1 reduce_sum.9
  62.9 2.8 %collective-permute-start.3 = (f32[5,2,128]{2,1,0:T(2,128)S(1)}, f32[5,2,128]{2,1,0:T(2,128)S(1)}, u32[]{:S(2)}, u32[]{:S(2)}) collective-permute-start(f32[5,2,128]{2,1,0:T(2,128)S(1)} %reduce_sum.9), channel_id=1, source_target_pairs={{0,384},{128,0},{256,128},{384,256},{1,385},{129,1},{257,129},{385... | collective-permute-start | bytes 15368 | tf_op jit(solution)/shard_map/ppermute | solution.py:201
  65.6 2.5 %collective-permute-start.2 = (f32[5,2,128]{2,1,0:T(2,128)S(1)}, f32[5,2,128]{2,1,0:T(2,128)S(1)}, u32[]{:S(2)}, u32[]{:S(2)}) collective-permute-start(f32[5,2,128]{2,1,0:T(2,128)S(1)} %reduce_sum.9), channel_id=1, source_target_pairs={{0,128},{128,256},{256,384},{384,0},{1,129},{129,257},{257,385},{3... | collective-permute-start | bytes 15368 | tf_op jit(solution)/shard_map/ppermute | solution.py:201
  68.1 2.5 %collective-permute-start.1 = (f32[5,2,128]{2,1,0:T(2,128)S(1)}, f32[5,2,128]{2,1,0:T(2,128)S(1)}, u32[]{:S(2)}, u32[]{:S(2)}) collective-permute-start(f32[5,2,128]{2,1,0:T(2,128)S(1)} %reduce_sum.9), channel_id=1, source_target_pairs={{0,256},{128,384},{256,0},{384,128},{1,257},{129,385},{257,1},{385... | collective-permute-start | bytes 15368 | tf_op jit(solution)/shard_map/ppermute | solution.py:201
  70.7 0.0 collective-permute-done.3
  70.7 0.5 collective-permute-done.2
  71.2 2.8 %collective-permute-done.1 = f32[5,2,128]{2,1,0:T(2,128)S(1)} collective-permute-done((f32[5,2,128]{2,1,0:T(2,128)S(1)}, f32[5,2,128]{2,1,0:T(2,128)S(1)}, u32[]{:S(2)}, u32[]{:S(2)}) %collective-permute-start.1) | collective-permute-done | bytes 5152 | tf_op jit(solution)/shard_map/ppermute | solution.py:201
  74.0 0.1 broadcast_in_dim.2
  74.1 18.6 %all_to_all.16 = f32[64,5,2,128]{3,2,1,0:T(2,128)S(1)} all-to-all(f32[64,5,2,128]{3,2,1,0:T(2,128)S(1)} %broadcast_in_dim.2), channel_id=1, replica_groups=mesh['x'=4,'y'=8,'z'=8,'core'=2] {'y','z'}, dimensions={0} | all-to-all | bytes 655360 | tf_op jit(solution)/shard_map/all_to_all | solution.py:213
  92.7 6.4 %collective-permute-start.4 = (f32[640,128]{1,0:T(8,128)S(1)}, f32[640,128]{1,0:T(8,128)S(1)}, u32[]{:S(2)}, u32[]{:S(2)}) collective-permute-start(f32[640,128]{1,0:T(8,128)S(1)} %bitcast.4), channel_id=1, source_target_pairs={{0,1},{1,0},{2,3},{3,2},{4,5},{5,4},{6,7},{7,6},{8,9},{9,8},{10,11... | collective-permute-start | bytes 983048 | tf_op jit(solution)/shard_map/ppermute | solution.py:196
  99.1 1.1 collective-permute-done.4.theirs
  100.2 15.4 %factor.1 = (f32[768,512]{1,0:T(8,128)}, f32[512,512]{1,0:T(8,128)}) custom-call(s32[1]{0:T(128)} %bitcast.core, f32[640,128]{1,0:T(8,128)S(1)} %bitcast.5, f32[640,128]{1,0:T(8,128)S(1)} %collective-permute-done.4.theirs, f32[4,768,128]{2,1,0:T(8,128)S(1)} %all-to-all-done.x), custom_call_target="tpu_custom_call" | custom-call | tf_op jit(solution)/shard_map/factor/pallas_call | solution.py:185
  (2 shorter events, 0.1 us)
Async XLA Ops:
  0.6 19.7 %all-to-all-start = ((f32[4,768,128]{2,1,0:T(8,128)}), f32[4,768,128]{2,1,0:T(8,128)S(1)}, u32[]{:S(2)}, u32[]{:S(2)}) async-start(f32[4,768,128]{2,1,0:T(8,128)} %bitcast.6), calls=%async_computation | async-start | bytes 3145728 | tf_op jit(solution)/shard_map/all_to_all | solution.py:220
  22.5 9.9 %collective-permute-start = (f32[640,128]{1,0:T(8,128)S(1)}, f32[640,128]{1,0:T(8,128)S(1)}, u32[]{:S(2)}, u32[]{:S(2)}) collective-permute-start(f32[640,128]{1,0:T(8,128)S(1)} %get-tuple-element.5), channel_id=1, source_target_pairs={{0,1},{1,0},{2,3},{3,2},{4,5},{5,4},{6,7},{7,6},{8,9},{9,8},{10,11... | collective-permute-start | bytes 983048 | tf_op jit(solution)/shard_map/ppermute | solution.py:196
  62.9 7.8 %collective-permute-start.3 = (f32[5,2,128]{2,1,0:T(2,128)S(1)}, f32[5,2,128]{2,1,0:T(2,128)S(1)}, u32[]{:S(2)}, u32[]{:S(2)}) collective-permute-start(f32[5,2,128]{2,1,0:T(2,128)S(1)} %reduce_sum.9), channel_id=1, source_target_pairs={{0,384},{128,0},{256,128},{384,256},{1,385},{129,1},{257,129},{385... | collective-permute-start | bytes 15368 | tf_op jit(solution)/shard_map/ppermute | solution.py:201
  65.6 5.6 %collective-permute-start.2 = (f32[5,2,128]{2,1,0:T(2,128)S(1)}, f32[5,2,128]{2,1,0:T(2,128)S(1)}, u32[]{:S(2)}, u32[]{:S(2)}) collective-permute-start(f32[5,2,128]{2,1,0:T(2,128)S(1)} %reduce_sum.9), channel_id=1, source_target_pairs={{0,128},{128,256},{256,384},{384,0},{1,129},{129,257},{257,385},{3... | collective-permute-start | bytes 15368 | tf_op jit(solution)/shard_map/ppermute | solution.py:201
  68.1 5.9 %collective-permute-start.1 = (f32[5,2,128]{2,1,0:T(2,128)S(1)}, f32[5,2,128]{2,1,0:T(2,128)S(1)}, u32[]{:S(2)}, u32[]{:S(2)}) collective-permute-start(f32[5,2,128]{2,1,0:T(2,128)S(1)} %reduce_sum.9), channel_id=1, source_target_pairs={{0,256},{128,384},{256,0},{384,128},{1,257},{129,385},{257,1},{385... | collective-permute-start | bytes 15368 | tf_op jit(solution)/shard_map/ppermute | solution.py:201
  92.7 7.4 %collective-permute-start.4 = (f32[640,128]{1,0:T(8,128)S(1)}, f32[640,128]{1,0:T(8,128)S(1)}, u32[]{:S(2)}, u32[]{:S(2)}) collective-permute-start(f32[640,128]{1,0:T(8,128)S(1)} %bitcast.4), channel_id=1, source_target_pairs={{0,1},{1,0},{2,3},{3,2},{4,5},{5,4},{6,7},{7,6},{8,9},{9,8},{10,11... | collective-permute-start | bytes 983048 | tf_op jit(solution)/shard_map/ppermute | solution.py:196

commit v3 on v2

--- a/solution.py
+++ b/solution.py
@@ -196,23 +196,19 @@
     return lax.ppermute(v, "core", [(0, 1), (1, 0)])
 
 
-def from_x(v, d):
-    count = lax.axis_size("x")
-    return lax.ppermute(v, "x", [(i, (i + d) % count) for i in range(count)])
-
-
 def all_sum(mine, theirs):
+    chips = ("x", "y", "z")
     mine = mine + other_core(theirs)
     rows = mine.shape[0]
-    peers = lax.axis_size(("y", "z"))
-    pieces = mine.reshape(peers, rows // peers // 2, 2, B)
-    pieces = lax.all_to_all(pieces, ("y", "z"), split_axis=0, concat_axis=0, tiled=True)
+    peers = lax.axis_size(chips)
+    share = -(-rows // peers)
+    pieces = jnp.concatenate([mine, jnp.zeros((share * peers - rows, B), F32)], 0).reshape(peers, share, 1, B)
+    pieces = lax.all_to_all(pieces, chips, split_axis=0, concat_axis=0, tiled=True)
     piece = jnp.sum(pieces, axis=0)
-    total = (piece + from_x(piece, 2)) + (from_x(piece, 1) + from_x(piece, 3))
-    pieces = jnp.broadcast_to(total[None], (peers,) + total.shape)
-    pieces = lax.all_to_all(pieces, ("y", "z"), split_axis=0, concat_axis=0, tiled=True)
-    mine = pieces.reshape(rows, B)
-    return mine, other_core(mine)
+    pieces = jnp.broadcast_to(piece[None], (peers,) + piece.shape)
+    pieces = lax.all_to_all(pieces, chips, split_axis=0, concat_axis=0, tiled=True)
+    mine = pieces.reshape(share * peers, B)
+    return mine[:rows], other_core(mine[:rows])
 
 
 def local(sketch):

time: 116 us -> 117 us (level)
  blocking collectives: 48.8 us -> 61.3 us
  starting transfers between devices: 27.7 us -> 19.2 us
  waiting for transfers between devices: 20.5 us -> 17.2 us
    all_to_all x2, blocking collectives: 48.8 us -> 61.3 us  [all_sum(): lax.all_to_all(pieces, chips, split_axis=0, concat_axis=0, tiled=True)]
    ppermute x3 -> x0, starting transfers between devices: 7.8 us -> none  [from_x(): return lax.ppermute(v, 'x', [(i, (i + d) % count) for i in range(count)])]
    ppermute x3 -> x0, waiting for transfers between devices: 3.32 us -> none  [from_x(): return lax.ppermute(v, 'x', [(i, (i + d) % count) for i in range(count)])]
  transfers between devices with their start and end apart: 6 -> 3, of which waited for: 5 -> 3; matrix products, arithmetic and copies ran while one was open for 0% -> 0% of each run, Pallas kernels for 0% -> 0%
where the time goes in v3:
time: 117 us
  blocking collectives  61.3 us (52%)
  starting transfers between devices  19.2 us (16%)
  Pallas kernels  17.6 us (15%)
  waiting for transfers between devices  17.2 us (15%)
    all_to_all x2, blocking collectives, all_sum(): lax.all_to_all(pieces, chips, split_axis=0, concat_axis=0, tiled=True)  61.3 us
    pallas_call x1, Pallas kernels, factor(): pl.pallas_call(factor_kernel, in_specs=[SMEM, VMEM, VMEM, VMEM], out_shap...  15.4 us
    all_to_all x1, waiting for transfers between devices, local(): lax.all_to_all(sketch.reshape(groups, -1, B), 'x', split_axis=0, concat_a...  14.9 us
    ppermute x2, starting transfers between devices, other_core(): return lax.ppermute(v, 'core', [(0, 1), (1, 0)])  14.4 us
    all_to_all x1, starting transfers between devices, local(): lax.all_to_all(sketch.reshape(groups, -1, B), 'x', split_axis=0, concat_a...  4.85 us
  transfers between devices with their start and end apart: 3, of which 3 were waited for; matrix products, arithmetic and copies ran while one was open for 0% of the time, Pallas kernels for 0%

profile of v3, /device:TPU:1, one launch (start us, length us, event | category | flops | bytes accessed | tf_op | source)
XLA Modules:
  0.0 116.6 jit_solution(17175209955809906341)
XLA Ops:
  0.6 4.9 %all-to-all-start = ((f32[4,768,128]{2,1,0:T(8,128)}), f32[4,768,128]{2,1,0:T(8,128)S(1)}, u32[]{:S(2)}, u32[]{:S(2)}) async-start(f32[4,768,128]{2,1,0:T(8,128)} %bitcast.4), calls=%async_computation | async-start | bytes 3145728 | tf_op jit(solution)/shard_map/all_to_all | solution.py:216
  5.5 14.9 %all-to-all-done.x = f32[4,768,128]{2,1,0:T(8,128)S(1)} async-done(((f32[4,768,128]{2,1,0:T(8,128)}), f32[4,768,128]{2,1,0:T(8,128)S(1)}, u32[]{:S(2)}, u32[]{:S(2)}) %all-to-all-start) | async-done | bytes 1572896 | tf_op jit(solution)/shard_map/all_to_all | solution.py:216
  20.4 2.2 %gram.1 = (f32[640,128]{1,0:T(8,128)S(1)}, f32[640,128]{1,0:T(8,128)S(1)}) custom-call(s32[1]{0:T(128)} %bitcast.core, f32[4,768,128]{2,1,0:T(8,128)S(1)} %all-to-all-done.x), custom_call_target="tpu_custom_call" | custom-call | tf_op jit(solution)/shard_map/gram/pallas_call | solution.py:123
  22.5 8.7 %collective-permute-start = (f32[640,128]{1,0:T(8,128)S(1)}, f32[640,128]{1,0:T(8,128)S(1)}, u32[]{:S(2)}, u32[]{:S(2)}) collective-permute-start(f32[640,128]{1,0:T(8,128)S(1)} %get-tuple-element.5), channel_id=1, source_target_pairs={{0,1},{1,0},{2,3},{3,2},{4,5},{5,4},{6,7},{7,6},{8,9},{9,8},{10,11... | collective-permute-start | bytes 983048 | tf_op jit(solution)/shard_map/ppermute | solution.py:196
  31.2 1.2 %collective-permute-done = f32[640,128]{1,0:T(8,128)S(1)} collective-permute-done((f32[640,128]{1,0:T(8,128)S(1)}, f32[640,128]{1,0:T(8,128)S(1)}, u32[]{:S(2)}, u32[]{:S(2)}) %collective-permute-start) | collective-permute-done | bytes 327712 | tf_op jit(solution)/shard_map/ppermute | solution.py:196
  32.6 36.1 %all_to_all.15 = f32[256,3,1,128]{3,2,1,0:T(1,128)S(1)} all-to-all(f32[256,3,1,128]{3,2,1,0:T(1,128)S(1)} %bitcast.5), channel_id=1, replica_groups=mesh['x'=4,'y'=8,'z'=8,'core'=2] {'x','y','z'}, dimensions={0} | all-to-all | bytes 786432 | tf_op jit(solution)/shard_map/all_to_all | solution.py:206
  68.7 0.3 reduce_sum.9
  69.0 0.2 broadcast_in_dim.2
  69.2 25.2 %all_to_all.16 = f32[256,3,1,128]{3,2,1,0:T(1,128)S(1)} all-to-all(f32[256,3,1,128]{3,2,1,0:T(1,128)S(1)} %broadcast_in_dim.2), channel_id=1, replica_groups=mesh['x'=4,'y'=8,'z'=8,'core'=2] {'x','y','z'}, dimensions={0} | all-to-all | bytes 786432 | tf_op jit(solution)/shard_map/all_to_all | solution.py:209
  94.4 5.7 %collective-permute-start.1 = (f32[640,128]{1,0:T(8,128)S(1)}, f32[640,128]{1,0:T(8,128)S(1)}, u32[]{:S(2)}, u32[]{:S(2)}) collective-permute-start(f32[640,128]{1,0:T(8,128)S(1)} %slice.5.mine), channel_id=1, source_target_pairs={{0,1},{1,0},{2,3},{3,2},{4,5},{5,4},{6,7},{7,6},{8,9},{9,8},{10,11... | collective-permute-start | bytes 983048 | tf_op jit(solution)/shard_map/ppermute | solution.py:196
  100.1 1.1 collective-permute-done.1.theirs
  101.2 15.4 %factor.1 = (f32[768,512]{1,0:T(8,128)}, f32[512,512]{1,0:T(8,128)}) custom-call(s32[1]{0:T(128)} %bitcast.core, f32[640,128]{1,0:T(8,128)S(1)} %slice.5.mine, f32[640,128]{1,0:T(8,128)S(1)} %collective-permute-done.1.theirs, f32[4,768,128]{2,1,0:T(8,128)S(1)} %all-to-all-done.x), custom_call_target="tpu_custom_call" | custom-call | tf_op jit(solution)/shard_map/factor/pallas_call | solution.py:185
  (3 shorter events, 0.1 us)
Async XLA Ops:
  0.6 19.7 %all-to-all-start = ((f32[4,768,128]{2,1,0:T(8,128)}), f32[4,768,128]{2,1,0:T(8,128)S(1)}, u32[]{:S(2)}, u32[]{:S(2)}) async-start(f32[4,768,128]{2,1,0:T(8,128)} %bitcast.4), calls=%async_computation | async-start | bytes 3145728 | tf_op jit(solution)/shard_map/all_to_all | solution.py:216
  22.5 9.9 %collective-permute-start = (f32[640,128]{1,0:T(8,128)S(1)}, f32[640,128]{1,0:T(8,128)S(1)}, u32[]{:S(2)}, u32[]{:S(2)}) collective-permute-start(f32[640,128]{1,0:T(8,128)S(1)} %get-tuple-element.5), channel_id=1, source_target_pairs={{0,1},{1,0},{2,3},{3,2},{4,5},{5,4},{6,7},{7,6},{8,9},{9,8},{10,11... | collective-permute-start | bytes 983048 | tf_op jit(solution)/shard_map/ppermute | solution.py:196
  94.4 6.8 %collective-permute-start.1 = (f32[640,128]{1,0:T(8,128)S(1)}, f32[640,128]{1,0:T(8,128)S(1)}, u32[]{:S(2)}, u32[]{:S(2)}) collective-permute-start(f32[640,128]{1,0:T(8,128)S(1)} %slice.5.mine), channel_id=1, source_target_pairs={{0,1},{1,0},{2,3},{3,2},{4,5},{5,4},{6,7},{7,6},{8,9},{9,8},{10,11... | collective-permute-start | bytes 983048 | tf_op jit(solution)/shard_map/ppermute | solution.py:196

commit v4 on v3

--- a/solution.py
+++ b/solution.py
@@ -12,7 +12,9 @@
 N = 512
 STEPS = N // B
 PAIRS = [(k, j) for k in range(STEPS) for j in range(k, STEPS)]
-HALF = len(PAIRS) // 2
+BOTH = 2
+HALF = (len(PAIRS) - BOTH) // 2
+OWN = BOTH + HALF
 F32 = jnp.float32
 BF16 = jnp.bfloat16
 NEAR = 3
@@ -20,16 +22,6 @@
 VMEM = pl.BlockSpec(memory_space=pltpu.VMEM)
 
 
-def dot(left, right, left_dim=1, right_dim=0):
-    return lax.dot_general(
-        left,
-        right,
-        (((left_dim,), (right_dim,)), ((), ())),
-        precision=lax.Precision.HIGHEST,
-        preferred_element_type=F32,
-    )
-
-
 def split(v):
     high = v.astype(BF16).astype(F32)
     rest = v - high
@@ -37,12 +29,22 @@
     return high, middle, rest - middle
 
 
+def lay_left(parts, dim):
+    a, b, c = parts
+    return jnp.concatenate([a, a, b, b, a, c], dim).astype(BF16)
+
+
+def lay_right(parts, dim):
+    a, b, c = parts
+    return jnp.concatenate([a, b, a, b, c, a], dim).astype(BF16)
+
+
+def parts_dot(left, right, left_dim=1, right_dim=0):
+    return lax.dot_general(left, right, (((left_dim,), (right_dim,)), ((), ())), preferred_element_type=F32)
+
+
 def wide_dot(left, right, left_dim, right_dim):
-    a, b, c = split(left)
-    d, e, f = split(right)
-    left = jnp.concatenate([a, a, b, b, a, c], left_dim).astype(BF16)
-    right = jnp.concatenate([d, e, d, e, f, d], right_dim).astype(BF16)
-    return lax.dot_general(left, right, (((left_dim,), (right_dim,)), ((), ())), preferred_element_type=F32)
+    return parts_dot(lay_left(split(left), left_dim), lay_right(split(right), right_dim), left_dim, right_dim)
 
 
 def factor_block(rows, after):
@@ -107,30 +109,53 @@
     return jnp.concatenate(upper, 0), jnp.concatenate(inverse, 0)
 
 
-def gram_kernel(scale, core, x, mine, theirs, parts):
-    wide = [jnp.concatenate([x[2 * h], x[2 * h + 1]], 1) for h in range(2)]
+def gram_kernel(scale, core, x, mine, theirs, x_parts, parts):
+    for h in range(STEPS // 2):
+        for i, part in enumerate(split(jnp.concatenate([x[2 * h], x[2 * h + 1]], 1))):
+            x_parts[i, :, 2 * h * B : 2 * h * B + 2 * B] = part.astype(BF16)
+    wide = [[x_parts[i, :, 2 * h * B : 2 * h * B + 2 * B] for i in range(3)] for h in range(STEPS // 2)]
+    turned = [lay_left([part.T for part in parts], 1) for parts in wide]
     for h, i in ((0, 0), (0, 1), (1, 1)):
-        product = dot(wide[h], wide[i], 0, 0) * scale
+        product = parts_dot(turned[h], lay_right(wide[i], 0)) * scale
         for k in (2 * h, 2 * h + 1):
             for j in (2 * i, 2 * i + 1):
                 if j >= k:
                     parts[PAIRS.index((k, j))] = product[k % 2 * B : k % 2 * B + B, j % 2 * B : j % 2 * B + B]
-    mine[...] = parts[pl.ds(core[0] * HALF, HALF)].reshape(HALF * B, B)
-    theirs[...] = parts[pl.ds((1 - core[0]) * HALF, HALF)].reshape(HALF * B, B)
+    for owner, out in ((core[0], mine), (1 - core[0], theirs)):
+        out[: BOTH * B, :] = parts[:BOTH].reshape(BOTH * B, B)
+        out[BOTH * B :, :] = parts[pl.ds(BOTH + owner * HALF, HALF)].reshape(HALF * B, B)
 
 
 def gram(core, x, scale):
     return pl.pallas_call(
         functools.partial(gram_kernel, scale),
         in_specs=[SMEM, VMEM],
-        out_shape=[jax.ShapeDtypeStruct((HALF * B, B), F32)] * 2,
+        out_shape=[jax.ShapeDtypeStruct((OWN * B, B), F32)] * 2 + [jax.ShapeDtypeStruct((3, x.shape[1], N), BF16)],
         scratch_shapes=[pltpu.VMEM((len(PAIRS), B, B), F32)],
         compiler_params=pltpu.CompilerParams(vmem_limit_bytes=32 << 20),
         name="gram",
     )(core, x)
 
 
-def factor_kernel(core, mine, theirs, x, basis_ref, u_ref, m):
+def first_kernel(mine, upper_ref, inverse_ref, panel_ref):
+    upper, inverse = factor_block([mine[8 * q : 8 * q + 8, :] for q in range(B // 8)], lambda p: None)
+    upper_ref[...] = upper
+    inverse_ref[...] = inverse
+    panel_ref[...] = wide_dot(inverse, mine[B : 2 * B, :], 1, 0)
+
+
+def first(mine):
+    return pl.pallas_call(
+        first_kernel,
+        in_specs=[VMEM],
+        out_shape=[jax.ShapeDtypeStruct((B, B), F32)] * 3,
+        compiler_params=pltpu.CompilerParams(vmem_limit_bytes=16 << 20),
+        cost_estimate=pl.CostEstimate(flops=4 << 20, bytes_accessed=4 << 20, transcendentals=0),
+        name="first",
+    )(mine)
+
+
+def factor_kernel(core, mine, theirs, upper0, inverse0, panel0, x, x_parts, basis_ref, u_ref, m, rest, right):
     todo = []
 
     def after(p):
@@ -150,46 +175,72 @@
         d = wide_dot(u_ref[block(k), block(i)], m[block(k), block(j)], 0, 0)
         m[block(i), block(j)] = -d if j == k else m[block(i), block(j)] - d
 
-    def basis(h, rows):
-        cols = slice(2 * h * B, 2 * h * B + 2 * B)
-        m[block(2 * h), block(2 * h + 1)] = jnp.zeros((B, B), F32)
-        left = jnp.concatenate([x[g, rows, :] for g in range(2 * h + 2)], 1)
-        basis_ref[rows, cols] = dot(left, m[cols, : cols.stop], 1, 1)
-
-    for k, j in PAIRS:
-        owner, at = divmod(PAIRS.index((k, j)), HALF)
-        m[block(k), block(j)] = jnp.where(core[0] == owner, mine[block(at), :], theirs[block(at), :])
+    def prepare(first_row, columns):
+        v = m[first_row : first_row + 2 * B, :columns]
+        right[:, : 6 * columns] = lay_right(split(v), 1)
+
+    def product(rows, columns):
+        left = lay_left([x_parts[i, rows, :columns] for i in range(3)], 1)
+        return parts_dot(left, right[:, : 6 * columns], 1, 1)
+
+    def basis_first(rows):
+        basis_ref[rows, : 2 * B] = product(rows, 2 * B)
+
+    def basis_last(rows):
+        both = product(rows, 3 * B)
+        basis_ref[rows, block(2)] = both[:, :B]
+        rest[rows, :] = both[:, B:] + x[3, rows, :]
+
+    chunks = [slice(c, c + 2 * B) for c in range(0, x.shape[1], 2 * B)]
+    for k, j in PAIRS[BOTH:]:
+        owner, at = divmod(PAIRS.index((k, j)) - BOTH, HALF)
+        m[block(k), block(j)] = jnp.where(core[0] == owner, mine[block(BOTH + at), :], theirs[block(at), :])
     for k in range(STEPS):
-        rows = [m[k * B + 8 * q : k * B + 8 * q + 8, block(k)] for q in range(B // 8)]
-        upper, inverse = factor_block(rows, after)
+        if k == 0:
+            upper, inverse = upper0[...], inverse0[...]
+        else:
+            rows = [m[k * B + 8 * q : k * B + 8 * q + 8, block(k)] for q in range(B // 8)]
+            upper, inverse = factor_block(rows, after)
         u_ref[block(k), block(k)] = upper
         for j in range(k):
             u_ref[block(k), block(j)] = jnp.zeros((B, B), F32)
+        if k == 0:
+            m[block(0), block(1)] = panel0[...]
+            u_ref[block(0), block(1)] = panel0[...]
+        elif k + 1 < STEPS:
+            panel(k, k + 1, inverse)
         if k + 1 < STEPS:
-            panel(k, k + 1, inverse)
             trail(k, k + 1, k + 1)
         m[block(k), block(k)] = inverse
-        todo += [functools.partial(panel, k, j, inverse) for j in range(STEPS) if j not in (k, k + 1)]
+        if k + 1 < STEPS:
+            todo += [functools.partial(panel, k, j, inverse) for j in range(STEPS) if j not in (k, k + 1)]
         for i in range(k + 1, STEPS):
             for j in range(STEPS):
                 if (j <= k or j >= i) and (i, j) != (k + 1, k + 1):
                     todo.append(functools.partial(trail, k, i, j))
-        if k == STEPS // 2:
-            todo += [functools.partial(basis, 0, slice(c, c + 2 * B)) for c in range(0, x.shape[1], 2 * B)]
-    todo += [functools.partial(basis, 1, slice(0, x.shape[1]))]
-    while todo:
-        todo.pop(0)()
-
-
-def factor(core, mine, theirs, x):
+        if k == 1:
+            m[block(0), block(1)] = jnp.zeros((B, B), F32)
+            todo.append(functools.partial(prepare, 0, 2 * B))
+            todo += [functools.partial(basis_first, rows) for rows in chunks]
+        if k == 2:
+            todo.append(functools.partial(prepare, 2 * B, 3 * B))
+            todo += [functools.partial(basis_last, rows) for rows in chunks]
+    basis_ref[:, block(3)] = wide_dot(rest[...], inverse, 1, 1)
+
+
+def factor(core, mine, theirs, upper0, inverse0, panel0, x, x_parts):
     return pl.pallas_call(
         factor_kernel,
-        in_specs=[SMEM, VMEM, VMEM, VMEM],
+        in_specs=[SMEM] + [VMEM] * 7,
         out_shape=[jax.ShapeDtypeStruct((x.shape[1], N), F32), jax.ShapeDtypeStruct((N, N), F32)],
-        scratch_shapes=[pltpu.VMEM((N, N), F32)],
+        scratch_shapes=[
+            pltpu.VMEM((N, N), F32),
+            pltpu.VMEM((x.shape[1], B), F32),
+            pltpu.VMEM((2 * B, 6 * 3 * B), BF16),
+        ],
         compiler_params=pltpu.CompilerParams(vmem_limit_bytes=32 << 20),
         name="factor",
-    )(core, mine, theirs, x)
+    )(core, mine, theirs, upper0, inverse0, panel0, x, x_parts)
 
 
 def other_core(v):
@@ -199,16 +250,13 @@
 def all_sum(mine, theirs):
     chips = ("x", "y", "z")
     mine = mine + other_core(theirs)
-    rows = mine.shape[0]
     peers = lax.axis_size(chips)
-    share = -(-rows // peers)
-    pieces = jnp.concatenate([mine, jnp.zeros((share * peers - rows, B), F32)], 0).reshape(peers, share, 1, B)
+    pieces = mine.reshape(peers, OWN * B // peers, 1, B)
     pieces = lax.all_to_all(pieces, chips, split_axis=0, concat_axis=0, tiled=True)
     piece = jnp.sum(pieces, axis=0)
     pieces = jnp.broadcast_to(piece[None], (peers,) + piece.shape)
     pieces = lax.all_to_all(pieces, chips, split_axis=0, concat_axis=0, tiled=True)
-    mine = pieces.reshape(share * peers, B)
-    return mine[:rows], other_core(mine[:rows])
+    return pieces.reshape(OWN * B, B)
 
 
 def local(sketch):
@@ -216,9 +264,10 @@
     x = lax.all_to_all(sketch.reshape(groups, -1, B), "x", split_axis=0, concat_axis=0, tiled=True)
     total_rows = x.shape[1] * lax.axis_size(("x", "y", "z", "core"))
     core = lax.axis_index("core").reshape(1)
-    mine, theirs = gram(core, x, 1.0 / total_rows)
-    mine, theirs = all_sum(mine, theirs)
-    return factor(core, mine, theirs, x)
+    mine, theirs, x_parts = gram(core, x, 1.0 / total_rows)
+    mine = all_sum(mine, theirs)
+    theirs = other_core(mine[BOTH * B :])
+    return factor(core, mine, theirs, *first(mine), x, x_parts)
 
 
 def solution(mesh):

time: 117 us -> 118 us (level)
  local copies, waits for them, and re-layouts: 0.26 us -> 3.29 us
    unnamed x0 -> x4, local copies, waits for them, and re-layouts: none -> 3.06 us
    pallas_call x1 -> x2, Pallas kernels: 15.4 us -> 14.8 us  [the longest x1 12 us: factor(): pl.pallas_call(factor_kernel, in_specs=[SMEM] + [VMEM] * 7, out_shape=[ja...]
  transfers between devices with their start and end apart: 3 -> 3, of which waited for: 3 -> 2; matrix products, arithmetic and copies ran while one was open for 0% -> 0% of each run, Pallas kernels for 0% -> 2%
where the time goes in v4:
time: 118 us
  blocking collectives  61.3 us (52%)
  starting transfers between devices  19.2 us (16%)
  Pallas kernels  16.9 us (14%)
  waiting for transfers between devices  16.2 us (14%)
  local copies, waits for them, and re-layouts  3.29 us (3%)
    all_to_all x2, blocking collectives, all_sum(): lax.all_to_all(pieces, chips, split_axis=0, concat_axis=0, tiled=True)  61.3 us
    all_to_all x1, waiting for transfers between devices, local(): lax.all_to_all(sketch.reshape(groups, -1, B), 'x', split_axis=0, concat_a...  14.9 us
    ppermute x2, starting transfers between devices, other_core(): return lax.ppermute(v, 'core', [(0, 1), (1, 0)])  14.4 us
    pallas_call x1, Pallas kernels, factor(): pl.pallas_call(factor_kernel, in_specs=[SMEM] + [VMEM] * 7, out_shape=[ja...  12 us
    all_to_all x1, starting transfers between devices, local(): lax.all_to_all(sketch.reshape(groups, -1, B), 'x', split_axis=0, concat_a...  4.85 us
    unnamed x4, local copies, waits for them, and re-layouts  3.06 us
    pallas_call x1, Pallas kernels, first(): pl.pallas_call(first_kernel, in_specs=[VMEM], out_shape=[jax.ShapeDtypeSt...  2.78 us
  transfers between devices with their start and end apart: 3, of which 2 were waited for; matrix products, arithmetic and copies ran while one was open for 0% of the time, Pallas kernels for 2%

profile of v4, /device:TPU:1, one launch (start us, length us, event | category | flops | bytes accessed | tf_op | source)
XLA Modules:
  0.0 118.0 jit_solution(16204792393962903548)
XLA Ops:
  0.6 4.9 %all-to-all-start = ((f32[4,768,128]{2,1,0:T(8,128)}), f32[4,768,128]{2,1,0:T(8,128)S(1)}, u32[]{:S(2)}, u32[]{:S(2)}) async-start(f32[4,768,128]{2,1,0:T(8,128)} %bitcast.7), calls=%async_computation | async-start | bytes 3145728 | tf_op jit(solution)/shard_map/all_to_all | solution.py:264
  5.5 14.9 %all-to-all-done.x = f32[4,768,128]{2,1,0:T(8,128)S(1)} async-done(((f32[4,768,128]{2,1,0:T(8,128)}), f32[4,768,128]{2,1,0:T(8,128)S(1)}, u32[]{:S(2)}, u32[]{:S(2)}) %all-to-all-start) | async-done | bytes 1572896 | tf_op jit(solution)/shard_map/all_to_all | solution.py:264
  20.4 2.1 %gram.1 = (f32[768,128]{1,0:T(8,128)S(1)}, f32[768,128]{1,0:T(8,128)S(1)}, bf16[3,768,512]{2,1,0:T(8,128)(2,1)S(1)}) custom-call(s32[1]{0:T(128)} %bitcast.core, f32[4,768,128]{2,1,0:T(8,128)S(1)} %all-to-all-done.x), custom_call_target="tpu_custom_call" | custom-call | tf_op jit(solution)/shard_map/gram/pallas_call | solution.py:130
  22.5 0.0 copy-start
  22.5 1.4 %copy-done = bf16[3,768,512]{2,1,0:T(8,128)(2,1)} copy-done((bf16[3,768,512]{2,1,0:T(8,128)(2,1)}, bf16[3,768,512]{2,1,0:T(8,128)(2,1)S(1)}, u32[]{:S(2)}) %copy-start) | copy-done | bytes 2359320
  23.9 8.7 %collective-permute-start = (f32[768,128]{1,0:T(8,128)S(1)}, f32[768,128]{1,0:T(8,128)S(1)}, u32[]{:S(2)}, u32[]{:S(2)}) collective-permute-start(f32[768,128]{1,0:T(8,128)S(1)} %get-tuple-element.9), channel_id=1, source_target_pairs={{0,1},{1,0},{2,3},{3,2},{4,5},{5,4},{6,7},{7,6},{8,9},{9,8},{10,11... | collective-permute-start | bytes 1179656 | tf_op jit(solution)/shard_map/ppermute | solution.py:247
  32.6 1.3 %collective-permute-done = f32[768,128]{1,0:T(8,128)S(1)} collective-permute-done((f32[768,128]{1,0:T(8,128)S(1)}, f32[768,128]{1,0:T(8,128)S(1)}, u32[]{:S(2)}, u32[]{:S(2)}) %collective-permute-start) | collective-permute-done | bytes 393248 | tf_op jit(solution)/shard_map/ppermute | solution.py:247
  33.9 0.1 add.3
  34.0 36.1 %all_to_all.15 = f32[256,3,1,128]{3,2,1,0:T(1,128)S(1)} all-to-all(f32[256,3,1,128]{3,2,1,0:T(1,128)S(1)} %bitcast.8), channel_id=1, replica_groups=mesh['x'=4,'y'=8,'z'=8,'core'=2] {'x','y','z'}, dimensions={0} | all-to-all | bytes 786432 | tf_op jit(solution)/shard_map/all_to_all | solution.py:255
  70.1 0.3 reduce_sum.9
  70.4 0.2 broadcast_in_dim.2
  70.6 25.2 %all_to_all.16 = f32[256,3,1,128]{3,2,1,0:T(1,128)S(1)} all-to-all(f32[256,3,1,128]{3,2,1,0:T(1,128)S(1)} %broadcast_in_dim.2), channel_id=1, replica_groups=mesh['x'=4,'y'=8,'z'=8,'core'=2] {'x','y','z'}, dimensions={0} | all-to-all | bytes 786432 | tf_op jit(solution)/shard_map/all_to_all | solution.py:258
  95.8 5.7 %collective-permute-start.1 = (f32[512,128]{1,0:T(8,128)S(1)}, f32[512,128]{1,0:T(8,128)S(1)}, u32[]{:S(2)}, u32[]{:S(2)}) collective-permute-start(f32[512,128]{1,0:T(8,128)S(1)} %slice.4), channel_id=1, source_target_pairs={{0,1},{1,0},{2,3},{3,2},{4,5},{5,4},{6,7},{7,6},{8,9},{9,8},{10,11... | collective-permute-start | bytes 786440 | tf_op jit(solution)/shard_map/ppermute | solution.py:247
  101.6 2.8 %first.1 = (f32[128,128]{1,0:T(8,128)S(1)}, f32[128,128]{1,0:T(8,128)S(1)}, f32[128,128]{1,0:T(8,128)S(1)}) custom-call(f32[768,128]{1,0:T(8,128)S(1)} %bitcast.5), custom_call_target="tpu_custom_call" | custom-call | flops 4194304 | bytes 4194304 | tf_op jit(solution)/shard_map/first/pallas_call | solution.py:148
  104.3 0.0 collective-permute-done.1.theirs
  104.3 0.0 copy-start.1
  104.4 1.7 %copy-done.1 = bf16[3,768,512]{2,1,0:T(8,128)(2,1)S(1)} copy-done((bf16[3,768,512]{2,1,0:T(8,128)(2,1)S(1)}, bf16[3,768,512]{2,1,0:T(8,128)(2,1)}, u32[]{:S(2)}) %copy-start.1) | copy-done | bytes 2359320
  106.0 12.0 %factor.1 = (f32[768,512]{1,0:T(8,128)}, f32[512,512]{1,0:T(8,128)}) custom-call(s32[1]{0:T(128)} %bitcast.core, f32[768,128]{1,0:T(8,128)S(1)} %bitcast.6, f32[512,128]{1,0:T(8,128)S(1)} %collective-permute-done.1.theirs, f32[128,128]{1,0:T(8,128)S(1)} %get-tuple-element.10.upper0, f32[128,128]{1,0:T(8,128)S(1)} %get-tuple-element.11.inverse0, ...), custom_call_target="tpu_custom_call" | custom-call | tf_op jit(solution)/shard_map/factor/pallas_call | solution.py:232
  (1 shorter events, 0.0 us)
Async XLA Ops:
  0.6 19.7 %all-to-all-start = ((f32[4,768,128]{2,1,0:T(8,128)}), f32[4,768,128]{2,1,0:T(8,128)S(1)}, u32[]{:S(2)}, u32[]{:S(2)}) async-start(f32[4,768,128]{2,1,0:T(8,128)} %bitcast.7), calls=%async_computation | async-start | bytes 3145728 | tf_op jit(solution)/shard_map/all_to_all | solution.py:264
  22.5 1.4 %copy-start = (bf16[3,768,512]{2,1,0:T(8,128)(2,1)}, bf16[3,768,512]{2,1,0:T(8,128)(2,1)S(1)}, u32[]{:S(2)}) copy-start(bf16[3,768,512]{2,1,0:T(8,128)(2,1)S(1)} %get-tuple-element.13.x_parts) | copy-start | bytes 7077892
  23.9 10.0 %collective-permute-start = (f32[768,128]{1,0:T(8,128)S(1)}, f32[768,128]{1,0:T(8,128)S(1)}, u32[]{:S(2)}, u32[]{:S(2)}) collective-permute-start(f32[768,128]{1,0:T(8,128)S(1)} %get-tuple-element.9), channel_id=1, source_target_pairs={{0,1},{1,0},{2,3},{3,2},{4,5},{5,4},{6,7},{7,6},{8,9},{9,8},{10,11... | collective-permute-start | bytes 1179656 | tf_op jit(solution)/shard_map/ppermute | solution.py:247
  95.8 8.5 %collective-permute-start.1 = (f32[512,128]{1,0:T(8,128)S(1)}, f32[512,128]{1,0:T(8,128)S(1)}, u32[]{:S(2)}, u32[]{:S(2)}) collective-permute-start(f32[512,128]{1,0:T(8,128)S(1)} %slice.4), channel_id=1, source_target_pairs={{0,1},{1,0},{2,3},{3,2},{4,5},{5,4},{6,7},{7,6},{8,9},{9,8},{10,11... | collective-permute-start | bytes 786440 | tf_op jit(solution)/shard_map/ppermute | solution.py:247
  104.3 1.7 %copy-start.1 = (bf16[3,768,512]{2,1,0:T(8,128)(2,1)S(1)}, bf16[3,768,512]{2,1,0:T(8,128)(2,1)}, u32[]{:S(2)}) copy-start(bf16[3,768,512]{2,1,0:T(8,128)(2,1)} %copy-done) | copy-start | bytes 7077892

commit v5 on v4

--- a/solution.py
+++ b/solution.py
@@ -130,8 +130,8 @@
     return pl.pallas_call(
         functools.partial(gram_kernel, scale),
         in_specs=[SMEM, VMEM],
-        out_shape=[jax.ShapeDtypeStruct((OWN * B, B), F32)] * 2 + [jax.ShapeDtypeStruct((3, x.shape[1], N), BF16)],
-        scratch_shapes=[pltpu.VMEM((len(PAIRS), B, B), F32)],
+        out_shape=[jax.ShapeDtypeStruct((OWN * B, B), F32)] * 2,
+        scratch_shapes=[pltpu.VMEM((3, x.shape[1], N), BF16), pltpu.VMEM((len(PAIRS), B, B), F32)],
         compiler_params=pltpu.CompilerParams(vmem_limit_bytes=32 << 20),
         name="gram",
     )(core, x)
@@ -155,7 +155,7 @@
     )(mine)
 
 
-def factor_kernel(core, mine, theirs, upper0, inverse0, panel0, x, x_parts, basis_ref, u_ref, m, rest, right):
+def factor_kernel(core, mine, theirs, upper0, inverse0, panel0, x, basis_ref, u_ref, m, rest, right, x_parts):
     todo = []
 
     def after(p):
@@ -174,6 +174,10 @@
     def trail(k, i, j):
         d = wide_dot(u_ref[block(k), block(i)], m[block(k), block(j)], 0, 0)
         m[block(i), block(j)] = -d if j == k else m[block(i), block(j)] - d
+
+    def separate(g, rows):
+        for i, part in enumerate(split(x[g, rows, :])):
+            x_parts[i, rows, block(g)] = part.astype(BF16)
 
     def prepare(first_row, columns):
         v = m[first_row : first_row + 2 * B, :columns]
@@ -218,6 +222,8 @@
             for j in range(STEPS):
                 if (j <= k or j >= i) and (i, j) != (k + 1, k + 1):
                     todo.append(functools.partial(trail, k, i, j))
+        if k == 0:
+            todo += [functools.partial(separate, g, rows) for g in range(STEPS - 1) for rows in chunks]
         if k == 1:
             m[block(0), block(1)] = jnp.zeros((B, B), F32)
             todo.append(functools.partial(prepare, 0, 2 * B))
@@ -228,19 +234,20 @@
     basis_ref[:, block(3)] = wide_dot(rest[...], inverse, 1, 1)
 
 
-def factor(core, mine, theirs, upper0, inverse0, panel0, x, x_parts):
+def factor(core, mine, theirs, upper0, inverse0, panel0, x):
     return pl.pallas_call(
         factor_kernel,
-        in_specs=[SMEM] + [VMEM] * 7,
+        in_specs=[SMEM] + [VMEM] * 6,
         out_shape=[jax.ShapeDtypeStruct((x.shape[1], N), F32), jax.ShapeDtypeStruct((N, N), F32)],
         scratch_shapes=[
             pltpu.VMEM((N, N), F32),
             pltpu.VMEM((x.shape[1], B), F32),
             pltpu.VMEM((2 * B, 6 * 3 * B), BF16),
+            pltpu.VMEM((3, x.shape[1], N), BF16),
         ],
         compiler_params=pltpu.CompilerParams(vmem_limit_bytes=32 << 20),
         name="factor",
-    )(core, mine, theirs, upper0, inverse0, panel0, x, x_parts)
+    )(core, mine, theirs, upper0, inverse0, panel0, x)
 
 
 def other_core(v):
@@ -264,10 +271,10 @@
     x = lax.all_to_all(sketch.reshape(groups, -1, B), "x", split_axis=0, concat_axis=0, tiled=True)
     total_rows = x.shape[1] * lax.axis_size(("x", "y", "z", "core"))
     core = lax.axis_index("core").reshape(1)
-    mine, theirs, x_parts = gram(core, x, 1.0 / total_rows)
+    mine, theirs = gram(core, x, 1.0 / total_rows)
     mine = all_sum(mine, theirs)
     theirs = other_core(mine[BOTH * B :])
-    return factor(core, mine, theirs, *first(mine), x, x_parts)
+    return factor(core, mine, theirs, *first(mine), x)
 
 
 def solution(mesh):

time: 118 us -> 115 us (0.975)
  local copies, waits for them, and re-layouts: 3.29 us -> 0.22 us
    unnamed x4 -> x0, local copies, waits for them, and re-layouts: 3.06 us -> none
where the time goes in v5:
time: 115 us
  blocking collectives  61.3 us (53%)
  starting transfers between devices  19.2 us (17%)
  Pallas kernels  17.1 us (15%)
  waiting for transfers between devices  16.2 us (14%)
    all_to_all x2, blocking collectives, all_sum(): lax.all_to_all(pieces, chips, split_axis=0, concat_axis=0, tiled=True)  61.3 us
    all_to_all x1, waiting for transfers between devices, local(): lax.all_to_all(sketch.reshape(groups, -1, B), 'x', split_axis=0, concat_a...  14.9 us
    ppermute x2, starting transfers between devices, other_core(): return lax.ppermute(v, 'core', [(0, 1), (1, 0)])  14.4 us
    pallas_call x1, Pallas kernels, factor(): pl.pallas_call(factor_kernel, in_specs=[SMEM] + [VMEM] * 6, out_shape=[ja...  12.2 us
    all_to_all x1, starting transfers between devices, local(): lax.all_to_all(sketch.reshape(groups, -1, B), 'x', split_axis=0, concat_a...  4.85 us
    pallas_call x1, Pallas kernels, first(): pl.pallas_call(first_kernel, in_specs=[VMEM], out_shape=[jax.ShapeDtypeSt...  2.78 us
  transfers between devices with their start and end apart: 3, of which 2 were waited for; matrix products, arithmetic and copies ran while one was open for 0% of the time, Pallas kernels for 2%

profile of v5, /device:TPU:1, one launch (start us, length us, event | category | flops | bytes accessed | tf_op | source)
XLA Modules:
  0.0 115.1 jit_solution(16399589643440686884)
XLA Ops:
  0.6 4.9 %all-to-all-start = ((f32[4,768,128]{2,1,0:T(8,128)}), f32[4,768,128]{2,1,0:T(8,128)S(1)}, u32[]{:S(2)}, u32[]{:S(2)}) async-start(f32[4,768,128]{2,1,0:T(8,128)} %bitcast.7), calls=%async_computation | async-start | bytes 3145728 | tf_op jit(solution)/shard_map/all_to_all | solution.py:271
  5.5 14.9 %all-to-all-done.x = f32[4,768,128]{2,1,0:T(8,128)S(1)} async-done(((f32[4,768,128]{2,1,0:T(8,128)}), f32[4,768,128]{2,1,0:T(8,128)S(1)}, u32[]{:S(2)}, u32[]{:S(2)}) %all-to-all-start) | async-done | bytes 1572896 | tf_op jit(solution)/shard_map/all_to_all | solution.py:271
  20.4 2.1 %gram.1 = (f32[768,128]{1,0:T(8,128)S(1)}, f32[768,128]{1,0:T(8,128)S(1)}) custom-call(s32[1]{0:T(128)} %bitcast.core, f32[4,768,128]{2,1,0:T(8,128)S(1)} %all-to-all-done.x), custom_call_target="tpu_custom_call" | custom-call | tf_op jit(solution)/shard_map/gram/pallas_call | solution.py:130
  22.4 8.7 %collective-permute-start = (f32[768,128]{1,0:T(8,128)S(1)}, f32[768,128]{1,0:T(8,128)S(1)}, u32[]{:S(2)}, u32[]{:S(2)}) collective-permute-start(f32[768,128]{1,0:T(8,128)S(1)} %get-tuple-element.8), channel_id=1, source_target_pairs={{0,1},{1,0},{2,3},{3,2},{4,5},{5,4},{6,7},{7,6},{8,9},{9,8},{10,11... | collective-permute-start | bytes 1179656 | tf_op jit(solution)/shard_map/ppermute | solution.py:254
  31.2 1.3 %collective-permute-done = f32[768,128]{1,0:T(8,128)S(1)} collective-permute-done((f32[768,128]{1,0:T(8,128)S(1)}, f32[768,128]{1,0:T(8,128)S(1)}, u32[]{:S(2)}, u32[]{:S(2)}) %collective-permute-start) | collective-permute-done | bytes 393248 | tf_op jit(solution)/shard_map/ppermute | solution.py:254
  32.5 0.1 add.3
  32.5 36.1 %all_to_all.15 = f32[256,3,1,128]{3,2,1,0:T(1,128)S(1)} all-to-all(f32[256,3,1,128]{3,2,1,0:T(1,128)S(1)} %bitcast.8), channel_id=1, replica_groups=mesh['x'=4,'y'=8,'z'=8,'core'=2] {'x','y','z'}, dimensions={0} | all-to-all | bytes 786432 | tf_op jit(solution)/shard_map/all_to_all | solution.py:262
  68.7 0.3 reduce_sum.9
  69.0 0.2 broadcast_in_dim.2
  69.2 25.2 %all_to_all.16 = f32[256,3,1,128]{3,2,1,0:T(1,128)S(1)} all-to-all(f32[256,3,1,128]{3,2,1,0:T(1,128)S(1)} %broadcast_in_dim.2), channel_id=1, replica_groups=mesh['x'=4,'y'=8,'z'=8,'core'=2] {'x','y','z'}, dimensions={0} | all-to-all | bytes 786432 | tf_op jit(solution)/shard_map/all_to_all | solution.py:265
  94.4 5.7 %collective-permute-start.1 = (f32[512,128]{1,0:T(8,128)S(1)}, f32[512,128]{1,0:T(8,128)S(1)}, u32[]{:S(2)}, u32[]{:S(2)}) collective-permute-start(f32[512,128]{1,0:T(8,128)S(1)} %slice.4), channel_id=1, source_target_pairs={{0,1},{1,0},{2,3},{3,2},{4,5},{5,4},{6,7},{7,6},{8,9},{9,8},{10,11... | collective-permute-start | bytes 786440 | tf_op jit(solution)/shard_map/ppermute | solution.py:254
  100.1 2.8 %first.1 = (f32[128,128]{1,0:T(8,128)S(1)}, f32[128,128]{1,0:T(8,128)S(1)}, f32[128,128]{1,0:T(8,128)S(1)}) custom-call(f32[768,128]{1,0:T(8,128)S(1)} %bitcast.5), custom_call_target="tpu_custom_call" | custom-call | flops 4194304 | bytes 4194304 | tf_op jit(solution)/shard_map/first/pallas_call | solution.py:148
  102.9 0.0 collective-permute-done.1.theirs
  102.9 12.2 %factor.1 = (f32[768,512]{1,0:T(8,128)}, f32[512,512]{1,0:T(8,128)}) custom-call(s32[1]{0:T(128)} %bitcast.core, f32[768,128]{1,0:T(8,128)S(1)} %bitcast.6, f32[512,128]{1,0:T(8,128)S(1)} %collective-permute-done.1.theirs, f32[128,128]{1,0:T(8,128)S(1)} %get-tuple-element.9.upper0, f32[128,128]{1,0:T(8,128)S(1)} %get-tuple-element.10.inverse0, ...), custom_call_target="tpu_custom_call" | custom-call | tf_op jit(solution)/shard_map/factor/pallas_call | solution.py:238
  (1 shorter events, 0.0 us)
Async XLA Ops:
  0.6 19.7 %all-to-all-start = ((f32[4,768,128]{2,1,0:T(8,128)}), f32[4,768,128]{2,1,0:T(8,128)S(1)}, u32[]{:S(2)}, u32[]{:S(2)}) async-start(f32[4,768,128]{2,1,0:T(8,128)} %bitcast.7), calls=%async_computation | async-start | bytes 3145728 | tf_op jit(solution)/shard_map/all_to_all | solution.py:271
  22.4 10.0 %collective-permute-start = (f32[768,128]{1,0:T(8,128)S(1)}, f32[768,128]{1,0:T(8,128)S(1)}, u32[]{:S(2)}, u32[]{:S(2)}) collective-permute-start(f32[768,128]{1,0:T(8,128)S(1)} %get-tuple-element.8), channel_id=1, source_target_pairs={{0,1},{1,0},{2,3},{3,2},{4,5},{5,4},{6,7},{7,6},{8,9},{9,8},{10,11... | collective-permute-start | bytes 1179656 | tf_op jit(solution)/shard_map/ppermute | solution.py:254
  94.4 8.5 %collective-permute-start.1 = (f32[512,128]{1,0:T(8,128)S(1)}, f32[512,128]{1,0:T(8,128)S(1)}, u32[]{:S(2)}, u32[]{:S(2)}) collective-permute-start(f32[512,128]{1,0:T(8,128)S(1)} %slice.4), channel_id=1, source_target_pairs={{0,1},{1,0},{2,3},{3,2},{4,5},{5,4},{6,7},{7,6},{8,9},{9,8},{10,11... | collective-permute-start | bytes 786440 | tf_op jit(solution)/shard_map/ppermute | solution.py:254

commit v6 on v5

--- a/solution.py
+++ b/solution.py
@@ -255,7 +255,7 @@
 
 
 def all_sum(mine, theirs):
-    chips = ("x", "y", "z")
+    chips = ("z", "y", "x")
     mine = mine + other_core(theirs)
     peers = lax.axis_size(chips)
     pieces = mine.reshape(peers, OWN * B // peers, 1, B)

time: 115 us -> 115 us (level)
  no operation moved by 1% of the time
where the time goes in v6:
time: 115 us
  blocking collectives  61 us (53%)
  starting transfers between devices  19.2 us (17%)
  Pallas kernels  17.1 us (15%)
  waiting for transfers between devices  16.2 us (14%)
    all_to_all x2, blocking collectives, all_sum(): lax.all_to_all(pieces, chips, split_axis=0, concat_axis=0, tiled=True)  61 us
    all_to_all x1, waiting for transfers between devices, local(): lax.all_to_all(sketch.reshape(groups, -1, B), 'x', split_axis=0, concat_a...  14.9 us
    ppermute x2, starting transfers between devices, other_core(): return lax.ppermute(v, 'core', [(0, 1), (1, 0)])  14.4 us
    pallas_call x1, Pallas kernels, factor(): pl.pallas_call(factor_kernel, in_specs=[SMEM] + [VMEM] * 6, out_shape=[ja...  12.2 us
    all_to_all x1, starting transfers between devices, local(): lax.all_to_all(sketch.reshape(groups, -1, B), 'x', split_axis=0, concat_a...  4.85 us
    pallas_call x1, Pallas kernels, first(): pl.pallas_call(first_kernel, in_specs=[VMEM], out_shape=[jax.ShapeDtypeSt...  2.78 us
  transfers between devices with their start and end apart: 3, of which 2 were waited for; matrix products, arithmetic and copies ran while one was open for 0% of the time, Pallas kernels for 2%

profile of v6, /device:TPU:1, one launch (start us, length us, event | category | flops | bytes accessed | tf_op | source)
XLA Modules:
  0.0 114.8 jit_solution(17754733560220449232)
XLA Ops:
  0.6 4.9 %all-to-all-start = ((f32[4,768,128]{2,1,0:T(8,128)}), f32[4,768,128]{2,1,0:T(8,128)S(1)}, u32[]{:S(2)}, u32[]{:S(2)}) async-start(f32[4,768,128]{2,1,0:T(8,128)} %bitcast.7), calls=%async_computation | async-start | bytes 3145728 | tf_op jit(solution)/shard_map/all_to_all | solution.py:271
  5.5 14.9 %all-to-all-done.x = f32[4,768,128]{2,1,0:T(8,128)S(1)} async-done(((f32[4,768,128]{2,1,0:T(8,128)}), f32[4,768,128]{2,1,0:T(8,128)S(1)}, u32[]{:S(2)}, u32[]{:S(2)}) %all-to-all-start) | async-done | bytes 1572896 | tf_op jit(solution)/shard_map/all_to_all | solution.py:271
  20.4 2.1 %gram.1 = (f32[768,128]{1,0:T(8,128)S(1)}, f32[768,128]{1,0:T(8,128)S(1)}) custom-call(s32[1]{0:T(128)} %bitcast.core, f32[4,768,128]{2,1,0:T(8,128)S(1)} %all-to-all-done.x), custom_call_target="tpu_custom_call" | custom-call | tf_op jit(solution)/shard_map/gram/pallas_call | solution.py:130
  22.4 8.7 %collective-permute-start = (f32[768,128]{1,0:T(8,128)S(1)}, f32[768,128]{1,0:T(8,128)S(1)}, u32[]{:S(2)}, u32[]{:S(2)}) collective-permute-start(f32[768,128]{1,0:T(8,128)S(1)} %get-tuple-element.8), channel_id=1, source_target_pairs={{0,1},{1,0},{2,3},{3,2},{4,5},{5,4},{6,7},{7,6},{8,9},{9,8},{10,11... | collective-permute-start | bytes 1179656 | tf_op jit(solution)/shard_map/ppermute | solution.py:254
  31.2 1.3 %collective-permute-done = f32[768,128]{1,0:T(8,128)S(1)} collective-permute-done((f32[768,128]{1,0:T(8,128)S(1)}, f32[768,128]{1,0:T(8,128)S(1)}, u32[]{:S(2)}, u32[]{:S(2)}) %collective-permute-start) | collective-permute-done | bytes 393248 | tf_op jit(solution)/shard_map/ppermute | solution.py:254
  32.5 0.1 add.3
  32.5 35.8 %all_to_all.15 = f32[256,3,1,128]{3,2,1,0:T(1,128)S(1)} all-to-all(f32[256,3,1,128]{3,2,1,0:T(1,128)S(1)} %bitcast.8), channel_id=1, replica_groups=mesh['x'=4,'y'=8,'z'=8,'core'=2] {'z','y','x'}, dimensions={0} | all-to-all | bytes 786432 | tf_op jit(solution)/shard_map/all_to_all | solution.py:262
  68.3 0.3 reduce_sum.9
  68.6 0.2 broadcast_in_dim.2
  68.8 25.2 %all_to_all.16 = f32[256,3,1,128]{3,2,1,0:T(1,128)S(1)} all-to-all(f32[256,3,1,128]{3,2,1,0:T(1,128)S(1)} %broadcast_in_dim.2), channel_id=1, replica_groups=mesh['x'=4,'y'=8,'z'=8,'core'=2] {'z','y','x'}, dimensions={0} | all-to-all | bytes 786432 | tf_op jit(solution)/shard_map/all_to_all | solution.py:265
  94.1 5.7 %collective-permute-start.1 = (f32[512,128]{1,0:T(8,128)S(1)}, f32[512,128]{1,0:T(8,128)S(1)}, u32[]{:S(2)}, u32[]{:S(2)}) collective-permute-start(f32[512,128]{1,0:T(8,128)S(1)} %slice.4), channel_id=1, source_target_pairs={{0,1},{1,0},{2,3},{3,2},{4,5},{5,4},{6,7},{7,6},{8,9},{9,8},{10,11... | collective-permute-start | bytes 786440 | tf_op jit(solution)/shard_map/ppermute | solution.py:254
  99.8 2.8 %first.1 = (f32[128,128]{1,0:T(8,128)S(1)}, f32[128,128]{1,0:T(8,128)S(1)}, f32[128,128]{1,0:T(8,128)S(1)}) custom-call(f32[768,128]{1,0:T(8,128)S(1)} %bitcast.5), custom_call_target="tpu_custom_call" | custom-call | flops 4194304 | bytes 4194304 | tf_op jit(solution)/shard_map/first/pallas_call | solution.py:148
  102.6 0.0 collective-permute-done.1.theirs
  102.6 12.2 %factor.1 = (f32[768,512]{1,0:T(8,128)}, f32[512,512]{1,0:T(8,128)}) custom-call(s32[1]{0:T(128)} %bitcast.core, f32[768,128]{1,0:T(8,128)S(1)} %bitcast.6, f32[512,128]{1,0:T(8,128)S(1)} %collective-permute-done.1.theirs, f32[128,128]{1,0:T(8,128)S(1)} %get-tuple-element.9.upper0, f32[128,128]{1,0:T(8,128)S(1)} %get-tuple-element.10.inverse0, ...), custom_call_target="tpu_custom_call" | custom-call | tf_op jit(solution)/shard_map/factor/pallas_call | solution.py:238
  (1 shorter events, 0.0 us)
Async XLA Ops:
  0.6 19.7 %all-to-all-start = ((f32[4,768,128]{2,1,0:T(8,128)}), f32[4,768,128]{2,1,0:T(8,128)S(1)}, u32[]{:S(2)}, u32[]{:S(2)}) async-start(f32[4,768,128]{2,1,0:T(8,128)} %bitcast.7), calls=%async_computation | async-start | bytes 3145728 | tf_op jit(solution)/shard_map/all_to_all | solution.py:271
  22.4 10.0 %collective-permute-start = (f32[768,128]{1,0:T(8,128)S(1)}, f32[768,128]{1,0:T(8,128)S(1)}, u32[]{:S(2)}, u32[]{:S(2)}) collective-permute-start(f32[768,128]{1,0:T(8,128)S(1)} %get-tuple-element.8), channel_id=1, source_target_pairs={{0,1},{1,0},{2,3},{3,2},{4,5},{5,4},{6,7},{7,6},{8,9},{9,8},{10,11... | collective-permute-start | bytes 1179656 | tf_op jit(solution)/shard_map/ppermute | solution.py:254
  94.1 8.5 %collective-permute-start.1 = (f32[512,128]{1,0:T(8,128)S(1)}, f32[512,128]{1,0:T(8,128)S(1)}, u32[]{:S(2)}, u32[]{:S(2)}) collective-permute-start(f32[512,128]{1,0:T(8,128)S(1)} %slice.4), channel_id=1, source_target_pairs={{0,1},{1,0},{2,3},{3,2},{4,5},{5,4},{6,7},{7,6},{8,9},{9,8},{10,11... | collective-permute-start | bytes 786440 | tf_op jit(solution)/shard_map/ppermute | solution.py:254

commit v7 on v6

--- a/solution.py
+++ b/solution.py
@@ -109,32 +109,33 @@
     return jnp.concatenate(upper, 0), jnp.concatenate(inverse, 0)
 
 
-def gram_kernel(scale, core, x, mine, theirs, x_parts, parts):
-    for h in range(STEPS // 2):
-        for i, part in enumerate(split(jnp.concatenate([x[2 * h], x[2 * h + 1]], 1))):
-            x_parts[i, :, 2 * h * B : 2 * h * B + 2 * B] = part.astype(BF16)
-    wide = [[x_parts[i, :, 2 * h * B : 2 * h * B + 2 * B] for i in range(3)] for h in range(STEPS // 2)]
-    turned = [lay_left([part.T for part in parts], 1) for parts in wide]
-    for h, i in ((0, 0), (0, 1), (1, 1)):
-        product = parts_dot(turned[h], lay_right(wide[i], 0)) * scale
-        for k in (2 * h, 2 * h + 1):
-            for j in (2 * i, 2 * i + 1):
-                if j >= k:
-                    parts[PAIRS.index((k, j))] = product[k % 2 * B : k % 2 * B + B, j % 2 * B : j % 2 * B + B]
-    for owner, out in ((core[0], mine), (1 - core[0], theirs)):
-        out[: BOTH * B, :] = parts[:BOTH].reshape(BOTH * B, B)
-        out[BOTH * B :, :] = parts[pl.ds(BOTH + owner * HALF, HALF)].reshape(HALF * B, B)
-
-
-def gram(core, x, scale):
+def gram_kernel(scale, owner, x, out):
+    def fill(pairs, start):
+        for k in range(STEPS):
+            columns = [j for i, j in pairs if i == k]
+            if columns:
+                left = lay_left([part.astype(BF16).T for part in split(x[k])], 1)
+                right = lay_right(split(jnp.concatenate([x[j] for j in columns], 1)), 0)
+                product = parts_dot(left, right) * scale
+                for n, j in enumerate(columns):
+                    at = (start + pairs.index((k, j))) * B
+                    out[at : at + B, :] = product[:, n * B : n * B + B]
+
+    fill(PAIRS[:BOTH], 0)
+    for which in range(2):
+        own = BOTH + which * HALF
+        pl.when(owner[0] == which)(functools.partial(fill, PAIRS[own : own + HALF], BOTH))
+
+
+def gram(owner, x, scale):
     return pl.pallas_call(
         functools.partial(gram_kernel, scale),
         in_specs=[SMEM, VMEM],
-        out_shape=[jax.ShapeDtypeStruct((OWN * B, B), F32)] * 2,
-        scratch_shapes=[pltpu.VMEM((3, x.shape[1], N), BF16), pltpu.VMEM((len(PAIRS), B, B), F32)],
+        out_shape=jax.ShapeDtypeStruct((OWN * B, B), F32),
         compiler_params=pltpu.CompilerParams(vmem_limit_bytes=32 << 20),
+        cost_estimate=pl.CostEstimate(flops=1 << 30, bytes_accessed=2 << 20, transcendentals=0),
         name="gram",
-    )(core, x)
+    )(owner, x)
 
 
 def first_kernel(mine, upper_ref, inverse_ref, panel_ref):
@@ -254,9 +255,8 @@
     return lax.ppermute(v, "core", [(0, 1), (1, 0)])
 
 
-def all_sum(mine, theirs):
+def all_sum(mine):
     chips = ("z", "y", "x")
-    mine = mine + other_core(theirs)
     peers = lax.axis_size(chips)
     pieces = mine.reshape(peers, OWN * B // peers, 1, B)
     pieces = lax.all_to_all(pieces, chips, split_axis=0, concat_axis=0, tiled=True)
@@ -271,8 +271,8 @@
     x = lax.all_to_all(sketch.reshape(groups, -1, B), "x", split_axis=0, concat_axis=0, tiled=True)
     total_rows = x.shape[1] * lax.axis_size(("x", "y", "z", "core"))
     core = lax.axis_index("core").reshape(1)
-    mine, theirs = gram(core, x, 1.0 / total_rows)
-    mine = all_sum(mine, theirs)
+    received = other_core(gram(1 - core, x, 1.0 / total_rows))
+    mine = all_sum(gram(core, x, 1.0 / total_rows) + received)
     theirs = other_core(mine[BOTH * B :])
     return factor(core, mine, theirs, *first(mine), x)
 

time: 115 us -> 115 us (level)
  waiting for transfers between devices: 16.2 us -> 14.9 us
    ppermute x2, waiting for transfers between devices: 1.33 us -> 0.01 us  [other_core(): return lax.ppermute(v, 'core', [(0, 1), (1, 0)])]
    pallas_call x1 -> x2, Pallas kernels: 2.08 us -> 3.05 us  [gram(): pl.pallas_call(functools.partial(gram_kernel, scale), in_specs=[SMEM, VME...]
  transfers between devices with their start and end apart: 3 -> 3, of which waited for: 2 -> 1; matrix products, arithmetic and copies ran while one was open for 0% -> 0% of each run, Pallas kernels for 2% -> 4%
where the time goes in v7:
time: 115 us
  blocking collectives  61.3 us (53%)
  starting transfers between devices  19.3 us (17%)
  Pallas kernels  18 us (16%)
  waiting for transfers between devices  14.9 us (13%)
    all_to_all x2, blocking collectives, all_sum(): lax.all_to_all(pieces, chips, split_axis=0, concat_axis=0, tiled=True)  61.3 us
    all_to_all x1, waiting for transfers between devices, local(): lax.all_to_all(sketch.reshape(groups, -1, B), 'x', split_axis=0, concat_a...  14.9 us
    ppermute x2, starting transfers between devices, other_core(): return lax.ppermute(v, 'core', [(0, 1), (1, 0)])  14.5 us
    pallas_call x1, Pallas kernels, factor(): pl.pallas_call(factor_kernel, in_specs=[SMEM] + [VMEM] * 6, out_shape=[ja...  12.2 us
    all_to_all x1, starting transfers between devices, local(): lax.all_to_all(sketch.reshape(groups, -1, B), 'x', split_axis=0, concat_a...  4.85 us
    pallas_call x2, Pallas kernels, gram(): pl.pallas_call(functools.partial(gram_kernel, scale), in_specs=[SMEM, VME...  3.05 us
    pallas_call x1, Pallas kernels, first(): pl.pallas_call(first_kernel, in_specs=[VMEM], out_shape=[jax.ShapeDtypeSt...  2.77 us
  transfers between devices with their start and end apart: 3, of which 1 were waited for; matrix products, arithmetic and copies ran while one was open for 0% of the time, Pallas kernels for 4%

profile of v7, /device:TPU:1, one launch (start us, length us, event | category | flops | bytes accessed | tf_op | source)
XLA Modules:
  0.0 114.8 jit_solution(8042361860679836382)
XLA Ops:
  0.6 4.9 %all-to-all-start = ((f32[4,768,128]{2,1,0:T(8,128)}), f32[4,768,128]{2,1,0:T(8,128)S(1)}, u32[]{:S(2)}, u32[]{:S(2)}) async-start(f32[4,768,128]{2,1,0:T(8,128)} %bitcast.7), calls=%async_computation | async-start | bytes 3145728 | tf_op jit(solution)/shard_map/all_to_all | solution.py:271
  5.5 14.9 %all-to-all-done.x = f32[4,768,128]{2,1,0:T(8,128)S(1)} async-done(((f32[4,768,128]{2,1,0:T(8,128)}), f32[4,768,128]{2,1,0:T(8,128)S(1)}, u32[]{:S(2)}, u32[]{:S(2)}) %all-to-all-start) | async-done | bytes 1572896 | tf_op jit(solution)/shard_map/all_to_all | solution.py:271
  20.4 1.4 %gram.3 = f32[768,128]{1,0:T(8,128)S(1)} custom-call(s32[1]{0:T(128)S(6)} %sub.3.owner, f32[4,768,128]{2,1,0:T(8,128)S(1)} %all-to-all-done.x), custom_call_target="tpu_custom_call" | custom-call | flops 1073741824 | bytes 2097152 | tf_op jit(solution)/shard_map/gram/pallas_call | solution.py:131
  21.8 9.0 %collective-permute-start = (f32[768,128]{1,0:T(8,128)S(1)}, f32[768,128]{1,0:T(8,128)S(1)}, u32[]{:S(2)}, u32[]{:S(2)}) collective-permute-start(f32[768,128]{1,0:T(8,128)S(1)} %gram.3), channel_id=1, source_target_pairs={{0,1},{1,0},{2,3},{3,2},{4,5},{5,4},{6,7},{7,6},{8,9},{9,8},{10,11... | collective-permute-start | bytes 1179656 | tf_op jit(solution)/shard_map/ppermute | solution.py:255
  30.7 1.7 %gram.2 = f32[768,128]{1,0:T(8,128)S(1)} custom-call(s32[1]{0:T(128)} %bitcast.owner.core, f32[4,768,128]{2,1,0:T(8,128)S(1)} %all-to-all-done.x), custom_call_target="tpu_custom_call" | custom-call | flops 1073741824 | bytes 2097152 | tf_op jit(solution)/shard_map/gram/pallas_call | solution.py:131
  32.4 0.0 collective-permute-done
  32.4 0.1 add.3
  32.5 36.3 %all_to_all.15 = f32[256,3,1,128]{3,2,1,0:T(1,128)S(1)} all-to-all(f32[256,3,1,128]{3,2,1,0:T(1,128)S(1)} %bitcast.8), channel_id=1, replica_groups=mesh['x'=4,'y'=8,'z'=8,'core'=2] {'z','y','x'}, dimensions={0} | all-to-all | bytes 786432 | tf_op jit(solution)/shard_map/all_to_all | solution.py:262
  68.8 0.3 reduce_sum.9
  69.1 0.2 broadcast_in_dim.2
  69.3 25.0 %all_to_all.16 = f32[256,3,1,128]{3,2,1,0:T(1,128)S(1)} all-to-all(f32[256,3,1,128]{3,2,1,0:T(1,128)S(1)} %broadcast_in_dim.2), channel_id=1, replica_groups=mesh['x'=4,'y'=8,'z'=8,'core'=2] {'z','y','x'}, dimensions={0} | all-to-all | bytes 786432 | tf_op jit(solution)/shard_map/all_to_all | solution.py:265
  94.4 5.5 %collective-permute-start.1 = (f32[512,128]{1,0:T(8,128)S(1)}, f32[512,128]{1,0:T(8,128)S(1)}, u32[]{:S(2)}, u32[]{:S(2)}) collective-permute-start(f32[512,128]{1,0:T(8,128)S(1)} %slice.4), channel_id=1, source_target_pairs={{0,1},{1,0},{2,3},{3,2},{4,5},{5,4},{6,7},{7,6},{8,9},{9,8},{10,11... | collective-permute-start | bytes 786440 | tf_op jit(solution)/shard_map/ppermute | solution.py:255
  99.8 2.8 %first.1 = (f32[128,128]{1,0:T(8,128)S(1)}, f32[128,128]{1,0:T(8,128)S(1)}, f32[128,128]{1,0:T(8,128)S(1)}) custom-call(f32[768,128]{1,0:T(8,128)S(1)} %bitcast.5), custom_call_target="tpu_custom_call" | custom-call | flops 4194304 | bytes 4194304 | tf_op jit(solution)/shard_map/first/pallas_call | solution.py:149
  102.6 0.0 collective-permute-done.1.theirs
  102.6 12.2 %factor.1 = (f32[768,512]{1,0:T(8,128)}, f32[512,512]{1,0:T(8,128)}) custom-call(s32[1]{0:T(128)} %bitcast.owner.core, f32[768,128]{1,0:T(8,128)S(1)} %bitcast.6, f32[512,128]{1,0:T(8,128)S(1)} %collective-permute-done.1.theirs, f32[128,128]{1,0:T(8,128)S(1)} %get-tuple-element.5.upper0, f32[128,128]{1,0:T(8,128)S(1)} %get-tuple-element.6.inverse0, ...), custom_call_target="tpu_custom_call" | custom-call | tf_op jit(solution)/shard_map/factor/pallas_call | solution.py:239
  (1 shorter events, 0.0 us)
Async XLA Ops:
  0.6 19.7 %all-to-all-start = ((f32[4,768,128]{2,1,0:T(8,128)}), f32[4,768,128]{2,1,0:T(8,128)S(1)}, u32[]{:S(2)}, u32[]{:S(2)}) async-start(f32[4,768,128]{2,1,0:T(8,128)} %bitcast.7), calls=%async_computation | async-start | bytes 3145728 | tf_op jit(solution)/shard_map/all_to_all | solution.py:271
  21.8 10.6 %collective-permute-start = (f32[768,128]{1,0:T(8,128)S(1)}, f32[768,128]{1,0:T(8,128)S(1)}, u32[]{:S(2)}, u32[]{:S(2)}) collective-permute-start(f32[768,128]{1,0:T(8,128)S(1)} %gram.3), channel_id=1, source_target_pairs={{0,1},{1,0},{2,3},{3,2},{4,5},{5,4},{6,7},{7,6},{8,9},{9,8},{10,11... | collective-permute-start | bytes 1179656 | tf_op jit(solution)/shard_map/ppermute | solution.py:255
  94.4 8.3 %collective-permute-start.1 = (f32[512,128]{1,0:T(8,128)S(1)}, f32[512,128]{1,0:T(8,128)S(1)}, u32[]{:S(2)}, u32[]{:S(2)}) collective-permute-start(f32[512,128]{1,0:T(8,128)S(1)} %slice.4), channel_id=1, source_target_pairs={{0,1},{1,0},{2,3},{3,2},{4,5},{5,4},{6,7},{7,6},{8,9},{9,8},{10,11... | collective-permute-start | bytes 786440 | tf_op jit(solution)/shard_map/ppermute | solution.py:255
